TPU v7x, 128 devices: a whole 4x4x4 slice. The times are simulated.
128 devices in a mesh: rows: 16 (over z, x), rep: 8 (over y, core).
Axes of the slice: x: 4, y: 4, z: 4, core: 2. Of those that a mesh axis runs over, the one named last changes fastest.
Arguments:
- grad_out: bfloat16 [163840, 512], P(('rows', 'rep')), may hold values from -6 to 6
- pre_act: bfloat16 [163840, 512], P(('rows', 'rep')), may hold values from -6 to 6
- features: bfloat16 [163840, 512], P(('rows', 'rep')), may hold values from -6 to 6
- weight: bfloat16 [512, 512], replicated, may hold values from -0.25 to 0.25
- edge_values: int32 [16, 8, 16, 18, 128, 128], P('rows', 'rep'), may hold values from 0 to 7
- row_tiles: int32 [16, 8, 16, 18], P('rows', 'rep'), may hold values from 0 to 79
- col_tiles: int32 [16, 8, 16, 18], P('rows', 'rep'), may hold values from 0 to 9
Outputs:
- input_grad: bfloat16 [163840, 512], P(('rows', 'rep'))
- weight_grad: float32 [512, 512], replicated
All inputs are finite; a program needn't handle non-finite values.
Results may differ from a plain program's by a relative error of at most 0.0049.
Values may be sent and summed in bfloat16 or wider, within the bound.
No kernel may reach another device: no remote copies, remote signals or barrier semaphores. Data moves between devices by JAX's collectives and lax.ppermute only.
A program may use at most 320 MiB of HBM per device.

v0:
```python
import functools

import jax
import jax.numpy as jnp
from jax import lax
from jax.experimental import pallas as pl
from jax.experimental.pallas import tpu as pltpu
from jax.sharding import PartitionSpec as P

LANE = 128
CHUNKS = ((0, 128), (128, 384))
BF16 = jnp.bfloat16
F32 = jnp.float32
VMEM_LIMIT = 56 * 1024 * 1024
SMALL = pl.CostEstimate(flops=0, bytes_accessed=1 << 16, transcendentals=0)


def plane_perm(dz, dx):
    return [(z * 4 + x, (z + dz) % 4 * 4 + (x + dx) % 4) for z in range(4) for x in range(4)]


XP, XM, X2 = plane_perm(0, 1), plane_perm(0, -1), plane_perm(0, 2)
ZP, ZM, Z2 = plane_perm(1, 0), plane_perm(-1, 0), plane_perm(2, 0)
CORE = [(i, i ^ 1) for i in range(8)]
YP, YM, Y2 = [[(i, (i + d) % 8) for i in range(8)] for d in (2, -2, 4)]


def rows_send(value, perm):
    return lax.ppermute(value, "rows", perm)


def rep_send(value, perm):
    return lax.ppermute(value, "rep", perm)


def mask_kernel(grad_ref, act_ref, upper_ref, lower_ref):
    half = upper_ref.shape[0]
    for rows, out_ref in ((pl.ds(0, half), upper_ref), (pl.ds(half, half), lower_ref)):
        kept = jnp.where(act_ref[rows].astype(F32) > 0, grad_ref[rows].astype(F32), 0.0)
        out_ref[...] = kept.astype(BF16)


def mask_call(grad_out, pre_act):
    rows, width = grad_out.shape
    return pl.pallas_call(
        mask_kernel,
        out_shape=[jax.ShapeDtypeStruct((rows // 2, width), BF16)] * 2,
        compiler_params=pltpu.CompilerParams(vmem_limit_bytes=VMEM_LIMIT),
        cost_estimate=SMALL,
        name="mask",
    )(grad_out, pre_act)


def prep_kernel(row_ref, values_ref, out_ref, degree_ref, *, per_step):
    step = pl.program_id(0)

    @pl.when(step == 0)
    def _():
        degree_ref[...] = jnp.zeros_like(degree_ref)

    ones = jnp.ones((8, LANE), BF16)
    for i in range(per_step):
        block = values_ref[i].astype(F32).astype(BF16)
        out_ref[i] = block
        sums = lax.dot_general(ones, block, (((1,), (1,)), ((), ())), preferred_element_type=F32)
        degree_ref[row_ref[step * per_step + i]] += sums


def prep_call(row_index, values, row_count):
    blocks = values.shape[0]
    per_step = 72
    return pl.pallas_call(
        functools.partial(prep_kernel, per_step=per_step),
        grid_spec=pltpu.PrefetchScalarGridSpec(
            num_scalar_prefetch=1,
            grid=(blocks // per_step,),
            in_specs=[pl.BlockSpec((per_step, LANE, LANE), lambda g, *_: (g, 0, 0))],
            out_specs=[
                pl.BlockSpec((per_step, LANE, LANE), lambda g, *_: (g, 0, 0)),
                pl.BlockSpec((row_count, 8, LANE), lambda g, *_: (0, 0, 0)),
            ],
        ),
        out_shape=[
            jax.ShapeDtypeStruct((blocks, LANE, LANE), BF16),
            jax.ShapeDtypeStruct((row_count, 8, LANE), F32),
        ],
        compiler_params=pltpu.CompilerParams(vmem_limit_bytes=VMEM_LIMIT),
        cost_estimate=SMALL,
        name="prep",
    )(row_index, values)


def product_kernel(index_ref, place_ref, values_ref, *refs, per_step, groups, group_tiles, begin):
    pieces, (part_ref, send_ref, held, total, staged, sem, out_sem) = refs[:10], refs[10:]
    step = pl.program_id(0)
    rows, width = held.shape[2:]
    half = rows // 2

    def copy_in(part, j, k):
        own, below, above, far_plus, far_minus = pieces[5 * part : 5 * part + 5]
        if j < 3:
            source, at = (own, below, above)[j], k * half
        else:
            source, at = (far_plus, far_minus)[k // 2], k % 2 * half
        z, x = (j, k) if part == 0 else (k, j)
        source = source.at[pl.ds(at, half), pl.ds(begin, width)]
        return pltpu.make_async_copy(source, held.at[z, x, pl.ds(part * half, half)], sem.at[part, z, x])

    @pl.when(step == 0)
    def _():
        for z in range(4):
            for x in range(4):
                copy_in(0, z, x).start()
                copy_in(1, x, z).start()
        total[...] = jnp.zeros_like(total)

    for z in range(4):

        @pl.when(step == z)
        def _(z=z):
            for x in range(4):
                copy_in(0, z, x).wait()
                copy_in(1, x, z).wait()

    first = place_ref[2 * groups + step] * per_step
    for i in range(per_step):
        at = first + i
        span = pl.ds(pl.multiple_of(index_ref[2, at] * LANE, LANE), LANE)
        source = held[step, index_ref[1, at], span, :]
        total[index_ref[0, at]] += jnp.dot(values_ref[i], source, preferred_element_type=F32)

    @pl.when(step == pl.num_programs(0) - 1)
    def _():
        staged[...] = total[...].astype(BF16)
        copies = [pltpu.make_async_copy(staged, part_ref, out_sem.at[groups])]
        for j in range(groups):
            other = pl.multiple_of(place_ref[groups + j] * group_tiles, group_tiles)
            copies.append(
                pltpu.make_async_copy(staged.at[pl.ds(other, group_tiles)], send_ref.at[j], out_sem.at[j])
            )
        for copy in copies:
            copy.start()
        for copy in copies:
            copy.wait()


def product_call(index, place, values, pieces, row_count, begin, width):
    blocks = values.shape[0]
    per_step, groups = blocks // 4, 4
    group_tiles = row_count // 8
    rows = pieces[0].shape[0] // 2
    return pl.pallas_call(
        functools.partial(
            product_kernel, per_step=per_step, groups=groups, group_tiles=group_tiles, begin=begin
        ),
        grid_spec=pltpu.PrefetchScalarGridSpec(
            num_scalar_prefetch=2,
            grid=(4,),
            in_specs=[pl.BlockSpec((per_step, LANE, LANE), lambda g, _, place: (place[2 * groups + g], 0, 0))]
            + [pl.BlockSpec(memory_space=pl.ANY)] * 10,
            out_specs=[pl.BlockSpec(memory_space=pl.ANY)] * 2,
            scratch_shapes=[
                pltpu.VMEM((4, 4, rows, width), BF16),
                pltpu.VMEM((row_count, LANE, width), F32),
                pltpu.VMEM((row_count, LANE, width), BF16),
                pltpu.SemaphoreType.DMA((2, 4, 4)),
                pltpu.SemaphoreType.DMA((groups + 1,)),
            ],
        ),
        out_shape=[
            jax.ShapeDtypeStruct((row_count, LANE, width), BF16),
            jax.ShapeDtypeStruct((groups, group_tiles, LANE, width), BF16),
        ],
        compiler_params=pltpu.CompilerParams(vmem_limit_bytes=VMEM_LIMIT),
        cost_estimate=SMALL,
        name="product",
    )(index, place, values, *pieces)


def halves_kernel(*refs):
    for source, target in zip(refs[:4], refs[4:]):
        target[...] = source[...]


def halves_call(*four):
    rows, width = four[0].shape
    steps = 4
    block = (rows // 2 // steps, width)
    low = pl.BlockSpec(block, lambda g: (g, 0))
    high = pl.BlockSpec(block, lambda g: (g + steps, 0))
    return pl.pallas_call(
        halves_kernel,
        grid=(steps,),
        in_specs=[low, high, low, high],
        out_specs=[low] * 4,
        out_shape=[jax.ShapeDtypeStruct((rows // 2, width), BF16)] * 4,
        compiler_params=pltpu.CompilerParams(vmem_limit_bytes=VMEM_LIMIT),
        cost_estimate=SMALL,
        name="halves",
    )(*four)


def pack_kernel(place_ref, part_ref, got_ref, *out_refs):
    side = pl.program_id(0)
    for i, out_ref in enumerate(out_refs):

        @pl.when(side == i)
        def _(out_ref=out_ref):
            out_ref[...] = (part_ref[...].astype(F32) + got_ref[0].astype(F32)).astype(BF16)


def pack_call(place, part, got):
    rest = got.shape[1:]
    out = pl.BlockSpec(rest, lambda g, _: (0, 0, 0))
    return pl.pallas_call(
        pack_kernel,
        grid_spec=pltpu.PrefetchScalarGridSpec(
            num_scalar_prefetch=1,
            grid=(3,),
            in_specs=[
                pl.BlockSpec(rest, lambda g, place: (place[g + 1], 0, 0)),
                pl.BlockSpec((1,) + rest, lambda g, _: (g + 1, 0, 0, 0)),
            ],
            out_specs=[out] * 3,
        ),
        out_shape=[jax.ShapeDtypeStruct(rest, BF16)] * 3,
        compiler_params=pltpu.CompilerParams(vmem_limit_bytes=VMEM_LIMIT),
        cost_estimate=SMALL,
        name="pack",
    )(place, part, got)


def gather_axis(value, me, send, perms):
    out = jnp.zeros((4,) + value.shape, value.dtype)
    parts = [send(value, p) for p in perms]
    for d, part in zip((0, 3, 1, 2), [value] + parts):
        out = lax.dynamic_update_index_in_dim(out, part, (me + d) % 4, 0)
    return out.reshape((4 * value.shape[0],) + value.shape[1:])


def exchange_axis(value, send, perms, dtype=BF16):
    value = value.astype(dtype)
    up, down, far = [send(value, p).astype(F32) for p in perms]
    return (value.astype(F32) + far) + (up + down)


def reduce_all(term, core, y, beside):
    rows = term.shape[0]
    halves = term.reshape(2, rows // 2, -1)
    other = lax.dynamic_index_in_dim(halves, 1 - core, 0, keepdims=False)
    mine = lax.dynamic_index_in_dim(halves, core, 0, keepdims=False)
    value = mine + rep_send(other, CORE)
    along_y = (YP, YM, Y2)
    value = value.reshape(4, rows // 8, -1)
    take = lambda i: lax.dynamic_index_in_dim(value, i % 4, 0, keepdims=False)
    parts = [rep_send(take(y + d).astype(BF16), p) for d, p in zip((1, 3, 2), along_y)]
    value = take(y) + parts[0].astype(F32) + parts[1].astype(F32) + parts[2].astype(F32)
    value = exchange_axis(value, rows_send, (ZP, ZM, Z2))
    value = exchange_axis(value, rows_send, (XP, XM, X2))
    value = after(value, beside)
    value = gather_axis(value, y, rep_send, along_y)
    got = rep_send(value, CORE)
    low = jnp.where(core == 0, value, got)
    high = jnp.where(core == 0, got, value)
    return jnp.concatenate([low, high])


def after(value, *others):
    return lax.optimization_barrier((value, others))[0]


def local(grad_out, pre_act, features, weight, edge_values, row_tiles, col_tiles):
    vert_rows, width = grad_out.shape
    sources = edge_values.shape[2]
    row_count = lax.axis_size("rep") * vert_rows // LANE
    total_verts = vert_rows * sources * lax.axis_size("rep")
    place = lax.axis_index("rows")
    rep = lax.axis_index("rep")
    z, x, y, core = place // 4, place % 4, rep // 2, rep % 2

    upper, lower = mask_call(grad_out, pre_act)
    block_features = lax.all_gather(features, "rep", axis=0, tiled=True)

    slot = jnp.array([0, 2, 3, 1], jnp.int32)
    span = jnp.arange(sources, dtype=jnp.int32)
    like = row_tiles[0, 0]
    wide = lambda v: jnp.broadcast_to(v[:, None], like.shape)
    source_x = slot[(span % 4 - x) % 4]
    index = jnp.stack([like, wide(source_x), col_tiles[0, 0]]).reshape(3, -1)
    along = (y + jnp.array([0, 1, 3, 2], jnp.int32)) % 4 * 2
    order = (z + jnp.array([0, 3, 1, 2], jnp.int32)) % 4
    groups = jnp.concatenate([along + core, along + 1 - core, order])

    values = after(edge_values.reshape(-1, LANE, LANE), upper, lower)
    values, degree = prep_call(like.reshape(-1), values, row_count)

    def spread(own, plus, minus, between):
        below, above = rows_send(own, plus), rows_send(own, minus)
        below, above = after(below, between), after(above, between)
        split = own.shape[0] // 2
        return own, below, above, rows_send(below[:split], plus), rows_send(above[split:], minus)

    first = [jnp.concatenate(spread(upper, XP, XM, values)), jnp.concatenate(spread(lower, ZP, ZM, values))]
    near = [rows_send(v, p) for v, ways in zip(first, ((ZP, ZM), (XP, XM))) for p in ways]
    far = [rows_send(v, p) for v, p in zip(halves_call(*near), (ZP, ZM, XP, XM))]
    pieces = [first[0], *near[:2], *far[:2], first[1], *near[2:], *far[2:]]

    degree = degree[:, 0]
    degree = degree + rep_send(degree, CORE)
    degree = exchange_axis(degree, rep_send, (YP, YM, Y2), F32)
    scale = lax.rsqrt(1.0 + degree)
    own_scale = lax.dynamic_index_in_dim(scale.reshape(8, vert_rows), rep, 0, keepdims=False)[:, None]
    norm = 1.0 / jnp.sqrt(jnp.float32(total_verts))
    scaled = (block_features.astype(F32) * (scale.reshape(-1, 1) * norm)).astype(BF16)

    sums, terms = [], []
    previous = (scaled, own_scale)
    for i, (begin, chunk) in enumerate(CHUNKS):
        made = product_call(after(index, previous), groups, values, pieces, row_count, begin, chunk)
        if i:
            made = after(made, sums[-1][2:])
        part, send = made
        got = rep_send(send, CORE)
        packed = pack_call(groups, part, got)
        sums.append([part, got] + [rep_send(v, p) for v, p in zip(packed, (YP, YM, Y2))])
        late = after(part, packed) if i else part
        terms.append(
            lax.dot_general(
                scaled,
                late.reshape(-1, chunk),
                (((0,), (0,)), ((), ())),
                preferred_element_type=F32,
            )
        )
        previous = packed
    weight_grad = reduce_all(jnp.concatenate(terms, axis=1), core, y, sums[-1][2:])

    aggregated = []
    for part, got, below, above, far in sums:
        own = lax.dynamic_slice_in_dim(part, rep * got.shape[1], got.shape[1], 0).astype(F32)
        own = own + got[0].astype(F32) + below.astype(F32) + above.astype(F32) + far.astype(F32)
        aggregated.append((own.reshape(vert_rows, -1) * own_scale).astype(BF16))
    input_grad = lax.dot_general(
        jnp.concatenate(aggregated, axis=1), weight, (((1,), (1,)), ((), ())), preferred_element_type=F32
    ).astype(BF16)
    return input_grad, weight_grad


def solution(mesh):
    return jax.shard_map(
        local,
        mesh=mesh,
        in_specs=(
            P(("rows", "rep"), None),
            P(("rows", "rep"), None),
            P(("rows", "rep"), None),
            P(),
            P("rows", "rep", None, None, None, None),
            P("rows", "rep", None, None),
            P("rows", "rep", None, None),
        ),
        out_specs=(P(("rows", "rep"), None), P()),
        check_vma=False,
    )
```

profile of v0, /device:TPU:1, one launch (start us, length us, event | category | flops | bytes accessed | tf_op | source)
XLA Modules:
  0.0 293.0 jit_solution(1414038900738671518)
XLA Ops:
  7.9 3.0 %mask.1 = (bf16[640,512]{1,0:T(8,128)(2,1)}, bf16[640,512]{1,0:T(8,128)(2,1)}) custom-call(bf16[1280,512]{1,0:T(8,128)(2,1)} %grad_ref.1, bf16[1280,512]{1,0:T(8,128)(2,1)} %act_ref.1), custom_call_target="tpu_custom_call" | custom-call | bytes 65536 | tf_op jit(solution)/shard_map/mask/pallas_call | solution.py:45
  10.9 2.5 collective-permute-start.10
  13.4 2.1 collective-permute-start.11
  16.7 1.5 collective-permute-start.5
  18.8 13.4 %prep.1 = (bf16[288,128,128]{2,1,0:T(8,128)(2,1)}, f32[80,8,128]{2,1,0:T(8,128)}) custom-call(s32[288]{0:T(512)} %reshape_squeeze.3.row_ref, s32[288,128,128]{2,1,0:T(8,128)} %bitcast.68), custom_call_target="tpu_custom_call" | custom-call | bytes 65536 | tf_op jit(solution)/shard_map/prep/pallas_call | solution.py:72
  33.5 2.7 collective-permute-start.13
  36.7 2.5 collective-permute-start.7
  44.7 2.2 collective-permute-start.15
  48.4 2.7 collective-permute-start.9
  52.1 3.9 %collective-permute-start = (f32[80,128]{1,0:T(8,128)S(1)}, f32[80,128]{1,0:T(8,128)S(1)}, u32[]{:S(2)}, u32[]{:S(2)}) collective-permute-start(f32[80,128]{1,0:T(8,128)S(1)} %bitcast.76), channel_id=1, source_target_pairs={{0,1},{1,0},{2,3},{3,2},{4,5},{5,4},{6,7},{7,6},{8,9},{9,8},{10,11... | collective-permute-start | bytes 122888 | tf_op jit(solution)/shard_map/ppermute | solution.py:33
  56.9 2.9 collective-permute-start.1
  60.8 1.8 collective-permute-done.1
  64.5 3.3 %collective-permute-done.2 = f32[80,128]{1,0:T(8,128)S(1)} collective-permute-done((f32[80,128]{1,0:T(8,128)S(1)}, f32[80,128]{1,0:T(8,128)S(1)}, u32[]{:S(2)}, u32[]{:S(2)}) %collective-permute-start.2) | collective-permute-done | bytes 40992 | tf_op jit(solution)/shard_map/ppermute | solution.py:33
  71.1 30.3 %collective-permute-done.14.refs_2_.refs_6_ = bf16[2560,512]{1,0:T(8,128)(2,1)S(1)} collective-permute-done((bf16[2560,512]{1,0:T(8,128)(2,1)}, bf16[2560,512]{1,0:T(8,128)(2,1)S(1)}, u32[]{:S(2)}, u32[]{:S(2)}) %collective-permute-start.14) | collective-permute-done | bytes 2621472 | tf_op jit(solution)/shard_map/ppermute | solution.py:29
  101.4 3.6 %collective-permute-done.8.refs_0_.refs_1_ = bf16[2560,512]{1,0:T(8,128)(2,1)} collective-permute-done((bf16[2560,512]{1,0:T(8,128)(2,1)}, bf16[2560,512]{1,0:T(8,128)(2,1)}, u32[]{:S(2)}, u32[]{:S(2)}) %collective-permute-start.8) | collective-permute-done | bytes 2621472 | tf_op jit(solution)/shard_map/ppermute | solution.py:29
  105.1 5.2 %halves.1 = (bf16[1280,512]{1,0:T(8,128)(2,1)}, bf16[1280,512]{1,0:T(8,128)(2,1)}, bf16[1280,512]{1,0:T(8,128)(2,1)}, bf16[1280,512]{1,0:T(8,128)(2,1)}) custom-call(bf16[2560,512]{1,0:T(8,128)(2,1)} %collective-permute-done.8.refs_0_.refs_1_, bf16[2560,512]{1,0:T(8,128)(2,1)} %collective-permute-done.9.refs_1_.refs_2_, bf16[2560,512]{1,0:T(8,128)(2,1)} %copy-done.2, ...), custom_call_target="tpu_custom_call" | custom-call | bytes 65536 | tf_op jit(solution)/shard_map/halves/pallas_call | solution.py:191
  110.3 2.7 collective-permute-start.17
  113.0 2.6 collective-permute-start.19
  115.6 10.6 %multiply_convert_fusion = bf16[10240,512]{1,0:T(8,128)(2,1)} fusion(bf16[10240,512]{1,0:T(8,128)(2,1)} %all-gather.2.cloned.1.call-done, f32[10240]{0:T(1024)S(1)} %get-tuple-element.60), kind=kLoop, calls=%fused_computation.1 | loop fusion | flops 15728640 | bytes 21012480 | tf_op jit(solution)/shard_map/convert_element_type | solution.py:314
  126.3 11.7 %collective-permute-done.16.refs_3_ = bf16[1280,512]{1,0:T(8,128)(2,1)S(1)} collective-permute-done((bf16[1280,512]{1,0:T(8,128)(2,1)}, bf16[1280,512]{1,0:T(8,128)(2,1)S(1)}, u32[]{:S(2)}, u32[]{:S(2)}) %collective-permute-start.16) | collective-permute-done | bytes 1310752 | tf_op jit(solution)/shard_map/ppermute | solution.py:29
  137.9 2.1 collective-permute-done.18.refs_8_
  140.1 11.2 %product.2 = (bf16[80,128,128]{2,1,0:T(8,128)(2,1)}, bf16[4,10,128,128]{3,2,1,0:T(8,128)(2,1)}) custom-call(s32[3,288]{1,0:T(4,128)} %pad_add_fusion.index_ref, s32[12]{0:T(128)} %pad_add_fusion.1.place_ref, bf16[288,128,128]{2,1,0:T(8,128)(2,1)} %get-tuple-element.36.values_ref, bf16[2560,512]{1,0:T(8,128)(2,1)} %constant_dynamic-update-slice_fusion.refs_0_, ...), custom_call_target="tpu_custom_call" | custom-call | bytes 65536 | tf_op jit(solution)/shard_map/product/pallas_call | solution.py:152
  151.2 5.7 %collective-permute-start.20 = (bf16[4,10,128,128]{3,2,1,0:T(8,128)(2,1)}, bf16[4,10,128,128]{3,2,1,0:T(8,128)(2,1)S(1)}, u32[]{:S(2)}, u32[]{:S(2)}) collective-permute-start(bf16[4,10,128,128]{3,2,1,0:T(8,128)(2,1)} %get-tuple-element.46), channel_id=1, source_target_pairs={{0,1},{1,0},{2,3},{3,2},{4,5},{5,4},{6,7},{7,6},{8,9},{9,8},{10,11... | collective-permute-start | bytes 3932168 | tf_op jit(solution)/shard_map/ppermute | solution.py:33
  156.9 2.9 collective-permute-done.20.got_ref
  160.9 4.0 %pack.2 = (bf16[10,128,128]{2,1,0:T(8,128)(2,1)}, bf16[10,128,128]{2,1,0:T(8,128)(2,1)}, bf16[10,128,128]{2,1,0:T(8,128)(2,1)}) custom-call(s32[12]{0:T(128)} %pad_add_fusion.1.place_ref, bf16[80,128,128]{2,1,0:T(8,128)(2,1)} %get-tuple-element.45.part_ref, bf16[4,10,128,128]{3,2,1,0:T(8,128)(2,1)} %copy-done.6), custom_call_target="tpu_custom_call" | custom-call | bytes 65536 | tf_op jit(solution)/shard_map/pack/pallas_call | solution.py:215
  165.9 1.7 collective-permute-start.22
  167.7 1.5 collective-permute-start.23
  169.2 18.4 %product.3 = (bf16[80,128,384]{2,1,0:T(8,128)(2,1)}, bf16[4,10,128,384]{3,2,1,0:T(8,128)(2,1)}) custom-call(s32[3,288]{1,0:T(4,128)} %pad_add_fusion.index_ref, s32[12]{0:T(128)} %pad_add_fusion.1.place_ref, bf16[288,128,128]{2,1,0:T(8,128)(2,1)} %get-tuple-element.36.values_ref, bf16[2560,512]{1,0:T(8,128)(2,1)} %constant_dynamic-update-slice_fusion.refs_0_, ...), custom_call_target="tpu_custom_call" | custom-call | bytes 65536 | tf_op jit(solution)/shard_map/product/pallas_call | solution.py:152
  187.6 1.5 collective-permute-start.24
  189.2 5.7 %fusion.25 = f32[512,128]{0,1:T(8,128)S(1)} fusion(bf16[10240,512]{1,0:T(8,128)(2,1)} %multiply_convert_fusion, bf16[10240,128]{1,0:T(8,128)(2,1)S(1)} %bitcast.72), kind=kOutput, calls=%fused_computation.78 | convolution fusion | flops 1342177280 | bytes 13369344 | tf_op jit(solution)/shard_map/dot_general | solution.py:328
  195.9 5.9 %pack.3 = (bf16[10,128,384]{2,1,0:T(8,128)(2,1)}, bf16[10,128,384]{2,1,0:T(8,128)(2,1)}, bf16[10,128,384]{2,1,0:T(8,128)(2,1)}) custom-call(s32[12]{0:T(128)} %pad_add_fusion.1.place_ref, bf16[80,128,384]{2,1,0:T(8,128)(2,1)} %get-tuple-element.58.part_ref, bf16[4,10,128,384]{3,2,1,0:T(8,128)(2,1)} %collective-permute-done.24.got_ref), custom_call_target="tpu_custom_call" | custom-call | bytes 65536 | tf_op jit(solution)/shard_map/pack/pallas_call | solution.py:215
  201.8 10.8 %fusion.26 = f32[512,384]{0,1:T(8,128)S(1)} fusion(bf16[10240,512]{1,0:T(8,128)(2,1)} %multiply_convert_fusion, bf16[10240,384]{1,0:T(8,128)(2,1)} %bitcast.69), kind=kOutput, calls=%fused_computation.79 | convolution fusion | flops 4026531840 | bytes 19136512 | tf_op jit(solution)/shard_map/dot_general | solution.py:328
  213.5 1.5 collective-permute-done.28
  215.7 2.2 collective-permute-start.30
  218.0 1.5 collective-permute-done.29
  219.6 3.0 %collective-permute-done.31 = bf16[64,512]{1,0:T(8,128)(2,1)S(1)} collective-permute-done((bf16[64,512]{1,0:T(8,128)(2,1)S(1)}, bf16[64,512]{1,0:T(8,128)(2,1)S(1)}, u32[]{:S(2)}, u32[]{:S(2)}) %collective-permute-start.31) | collective-permute-done | bytes 65568 | tf_op jit(solution)/shard_map/ppermute | solution.py:33
  224.4 1.8 collective-permute-start.34
  226.3 2.7 collective-permute-start.26
  230.3 1.5 fusion.9
  231.8 2.1 collective-permute-start.36
  233.9 2.5 collective-permute-start.37
  238.0 10.1 %collective-permute-done.25 = bf16[10,128,384]{2,1,0:T(8,128)(2,1)S(1)} collective-permute-done((bf16[10,128,384]{2,1,0:T(8,128)(2,1)}, bf16[10,128,384]{2,1,0:T(8,128)(2,1)S(1)}, u32[]{:S(2)}, u32[]{:S(2)}) %collective-permute-start.25) | collective-permute-done | bytes 983072 | tf_op jit(solution)/shard_map/ppermute | solution.py:33
  248.1 21.1 %collective-permute-done.27 = bf16[10,128,384]{2,1,0:T(8,128)(2,1)S(1)} collective-permute-done((bf16[10,128,384]{2,1,0:T(8,128)(2,1)}, bf16[10,128,384]{2,1,0:T(8,128)(2,1)S(1)}, u32[]{:S(2)}, u32[]{:S(2)}) %collective-permute-start.27) | collective-permute-done | bytes 983072 | tf_op jit(solution)/shard_map/ppermute | solution.py:33
  269.7 2.1 collective-permute-start.39
  271.9 2.1 fusion.2
  275.2 2.0 collective-permute-done.40
  277.2 5.6 %collective-permute-start.41 = (f32[256,512]{1,0:T(8,128)S(1)}, f32[256,512]{1,0:T(8,128)S(1)}, u32[]{:S(2)}, u32[]{:S(2)}) collective-permute-start(f32[256,512]{1,0:T(8,128)S(1)} %bitcast.73), channel_id=1, source_target_pairs={{0,1},{1,0},{2,3},{3,2},{4,5},{5,4},{6,7},{7,6},{8,9},{9,8},{10,11... | collective-permute-start | bytes 1572872 | tf_op jit(solution)/shard_map/ppermute | solution.py:33
  283.1 1.9 convolution_convert_fusion
  (125 shorter events, 32.4 us)
Async XLA Ops:
  7.2 275.9 %copy-start = (bf16[512,512]{1,0:T(8,128)(2,1)S(1)}, bf16[512,512]{1,0:T(8,128)(2,1)}, u32[]{:S(2)}) copy-start(bf16[512,512]{1,0:T(8,128)(2,1)} %param.13) | copy-start | bytes 1572868
  7.2 108.5 %all-gather.2.cloned.1.call-start = ((), (), s32[]{:S(2)}) async-start(), calls=%async_computation | async-start | bytes 11796480 | tf_op jit(solution)/shard_map/all_gather | solution.py:282
  10.9 22.5 %collective-permute-start.10 = (bf16[640,512]{1,0:T(8,128)(2,1)}, bf16[640,512]{1,0:T(8,128)(2,1)S(1)}, u32[]{:S(2)}, u32[]{:S(2)}) collective-permute-start(bf16[640,512]{1,0:T(8,128)(2,1)} %get-tuple-element.32), channel_id=1, source_target_pairs={{0,32},{8,40},{16,48},{24,56},{32,64},{40,72},{48,80},{56,88},{64,... | collective-permute-start | bytes 1966088 | tf_op jit(solution)/shard_map/ppermute | solution.py:29
  13.4 20.0 %collective-permute-start.11 = (bf16[640,512]{1,0:T(8,128)(2,1)}, bf16[640,512]{1,0:T(8,128)(2,1)S(1)}, u32[]{:S(2)}, u32[]{:S(2)}) collective-permute-start(bf16[640,512]{1,0:T(8,128)(2,1)} %get-tuple-element.32), channel_id=1, source_target_pairs={{0,96},{8,104},{16,112},{24,120},{32,0},{40,8},{48,16},{56,24},{64... | collective-permute-start | bytes 1966088 | tf_op jit(solution)/shard_map/ppermute | solution.py:29
  15.5 20.8 %collective-permute-start.4 = (bf16[640,512]{1,0:T(8,128)(2,1)}, bf16[640,512]{1,0:T(8,128)(2,1)S(1)}, u32[]{:S(2)}, u32[]{:S(2)}) collective-permute-start(bf16[640,512]{1,0:T(8,128)(2,1)} %get-tuple-element.31), channel_id=1, source_target_pairs={{0,8},{8,16},{16,24},{24,0},{32,40},{40,48},{48,56},{56,32},{64,72... | collective-permute-start | bytes 1966088 | tf_op jit(solution)/shard_map/ppermute | solution.py:29
  16.7 19.6 %collective-permute-start.5 = (bf16[640,512]{1,0:T(8,128)(2,1)}, bf16[640,512]{1,0:T(8,128)(2,1)S(1)}, u32[]{:S(2)}, u32[]{:S(2)}) collective-permute-start(bf16[640,512]{1,0:T(8,128)(2,1)} %get-tuple-element.31), channel_id=1, source_target_pairs={{0,24},{8,0},{16,8},{24,16},{32,56},{40,32},{48,40},{56,48},{64,88... | collective-permute-start | bytes 1966088 | tf_op jit(solution)/shard_map/ppermute | solution.py:29
  33.4 9.3 %collective-permute-start.12 = (bf16[320,512]{1,0:T(8,128)(2,1)S(1)}, bf16[320,512]{1,0:T(8,128)(2,1)S(1)}, u32[]{:S(2)}, u32[]{:S(2)}) collective-permute-start(bf16[320,512]{1,0:T(8,128)(2,1)S(1)} %slice.24), channel_id=1, source_target_pairs={{0,32},{8,40},{16,48},{24,56},{32,64},{40,72},{48,80},{56,88},{64,... | collective-permute-start | bytes 983048 | tf_op jit(solution)/shard_map/ppermute | solution.py:29
  33.5 9.9 %collective-permute-start.13 = (bf16[320,512]{1,0:T(8,128)(2,1)S(1)}, bf16[320,512]{1,0:T(8,128)(2,1)S(1)}, u32[]{:S(2)}, u32[]{:S(2)}) collective-permute-start(bf16[320,512]{1,0:T(8,128)(2,1)S(1)} %slice.25), channel_id=1, source_target_pairs={{0,96},{8,104},{16,112},{24,120},{32,0},{40,8},{48,16},{56,24},{64... | collective-permute-start | bytes 983048 | tf_op jit(solution)/shard_map/ppermute | solution.py:29
  36.3 10.6 %collective-permute-start.6 = (bf16[320,512]{1,0:T(8,128)(2,1)S(1)}, bf16[320,512]{1,0:T(8,128)(2,1)S(1)}, u32[]{:S(2)}, u32[]{:S(2)}) collective-permute-start(bf16[320,512]{1,0:T(8,128)(2,1)S(1)} %slice.22), channel_id=1, source_target_pairs={{0,8},{8,16},{16,24},{24,0},{32,40},{40,48},{48,56},{56,32},{64,72... | collective-permute-start | bytes 983048 | tf_op jit(solution)/shard_map/ppermute | solution.py:29
  36.7 11.0 %collective-permute-start.7 = (bf16[320,512]{1,0:T(8,128)(2,1)S(1)}, bf16[320,512]{1,0:T(8,128)(2,1)S(1)}, u32[]{:S(2)}, u32[]{:S(2)}) collective-permute-start(bf16[320,512]{1,0:T(8,128)(2,1)S(1)} %slice.23), channel_id=1, source_target_pairs={{0,24},{8,0},{16,8},{24,16},{32,56},{40,32},{48,40},{56,48},{64,88... | collective-permute-start | bytes 983048 | tf_op jit(solution)/shard_map/ppermute | solution.py:29
  40.9 15.1 %copy-start.12 = (s32[4]{0:T(128)S(1)}, s32[4]{0:T(128)}, u32[]{:S(2)}) copy-start(s32[4]{0:T(128)} %constant.159.clone) | copy-start | bytes 52
  40.9 18.9 %copy-start.1 = (s32[4]{0:T(128)S(1)}, s32[4]{0:T(128)}, u32[]{:S(2)}) copy-start(s32[4]{0:T(128)} %constant.157.clone) | copy-start | bytes 52
  41.8 18.9 %copy-start.10 = (s32[1,1,16,18]{3,2,1,0:T(8,128)S(1)}, s32[1,1,16,18]{3,2,1,0:T(8,128)}, u32[]{:S(2)}) copy-start(s32[1,1,16,18]{3,2,1,0:T(8,128)} %param.16) | copy-start | bytes 3460
  44.2 57.2 %collective-permute-start.14 = (bf16[2560,512]{1,0:T(8,128)(2,1)}, bf16[2560,512]{1,0:T(8,128)(2,1)S(1)}, u32[]{:S(2)}, u32[]{:S(2)}) collective-permute-start(bf16[2560,512]{1,0:T(8,128)(2,1)} %constant_dynamic-update-slice_fusion.5.refs_5_), channel_id=1, source_target_pairs={{0,8},{8,16},{16,24},{24,0},{32,40},{40,48},{48,56},{56,32},{64,72... | collective-permute-start | bytes 7864328 | tf_op jit(solution)/shard_map/ppermute | solution.py:29
  44.7 56.7 %collective-permute-start.15 = (bf16[2560,512]{1,0:T(8,128)(2,1)}, bf16[2560,512]{1,0:T(8,128)(2,1)}, u32[]{:S(2)}, u32[]{:S(2)}) collective-permute-start(bf16[2560,512]{1,0:T(8,128)(2,1)} %constant_dynamic-update-slice_fusion.5.refs_5_), channel_id=1, source_target_pairs={{0,24},{8,0},{16,8},{24,16},{32,56},{40,32},{48,40},{56,48},{64,88... | collective-permute-start | bytes 7864328 | tf_op jit(solution)/shard_map/ppermute | solution.py:29
  48.4 56.6 %collective-permute-start.8 = (bf16[2560,512]{1,0:T(8,128)(2,1)}, bf16[2560,512]{1,0:T(8,128)(2,1)}, u32[]{:S(2)}, u32[]{:S(2)}) collective-permute-start(bf16[2560,512]{1,0:T(8,128)(2,1)} %constant_dynamic-update-slice_fusion.refs_0_), channel_id=1, source_target_pairs={{0,32},{8,40},{16,48},{24,56},{32,64},{40,72},{48,80},{56,88},{64,... | collective-permute-start | bytes 7864328 | tf_op jit(solution)/shard_map/ppermute | solution.py:29
  48.4 56.6 %collective-permute-start.9 = (bf16[2560,512]{1,0:T(8,128)(2,1)}, bf16[2560,512]{1,0:T(8,128)(2,1)}, u32[]{:S(2)}, u32[]{:S(2)}) collective-permute-start(bf16[2560,512]{1,0:T(8,128)(2,1)} %constant_dynamic-update-slice_fusion.refs_0_), channel_id=1, source_target_pairs={{0,96},{8,104},{16,112},{24,120},{32,0},{40,8},{48,16},{56,24},{64... | collective-permute-start | bytes 7864328 | tf_op jit(solution)/shard_map/ppermute | solution.py:29
  52.1 4.8 %collective-permute-start = (f32[80,128]{1,0:T(8,128)S(1)}, f32[80,128]{1,0:T(8,128)S(1)}, u32[]{:S(2)}, u32[]{:S(2)}) collective-permute-start(f32[80,128]{1,0:T(8,128)S(1)} %bitcast.76), channel_id=1, source_target_pairs={{0,1},{1,0},{2,3},{3,2},{4,5},{5,4},{6,7},{7,6},{8,9},{9,8},{10,11... | collective-permute-start | bytes 122888 | tf_op jit(solution)/shard_map/ppermute | solution.py:33
  56.9 5.7 %collective-permute-start.1 = (f32[80,128]{1,0:T(8,128)S(1)}, f32[80,128]{1,0:T(8,128)S(1)}, u32[]{:S(2)}, u32[]{:S(2)}) collective-permute-start(f32[80,128]{1,0:T(8,128)S(1)} %add.212), channel_id=1, source_target_pairs={{0,4},{1,5},{2,6},{3,7},{4,0},{5,1},{6,2},{7,3},{8,12},{9,13},{10,... | collective-permute-start | bytes 122888 | tf_op jit(solution)/shard_map/ppermute | solution.py:33
  62.5 5.3 %collective-permute-start.2 = (f32[80,128]{1,0:T(8,128)S(1)}, f32[80,128]{1,0:T(8,128)S(1)}, u32[]{:S(2)}, u32[]{:S(2)}) collective-permute-start(f32[80,128]{1,0:T(8,128)S(1)} %add.212), channel_id=1, source_target_pairs={{0,2},{1,3},{2,4},{3,5},{4,6},{5,7},{6,0},{7,1},{8,10},{9,11},{10,... | collective-permute-start | bytes 122888 | tf_op jit(solution)/shard_map/ppermute | solution.py:33
  67.8 3.3 %collective-permute-start.3 = (f32[80,128]{1,0:T(8,128)S(1)}, f32[80,128]{1,0:T(8,128)S(1)}, u32[]{:S(2)}, u32[]{:S(2)}) collective-permute-start(f32[80,128]{1,0:T(8,128)S(1)} %add.212), channel_id=1, source_target_pairs={{0,6},{1,7},{2,0},{3,1},{4,2},{5,3},{6,4},{7,5},{8,14},{9,15},{10,... | collective-permute-start | bytes 122888 | tf_op jit(solution)/shard_map/ppermute | solution.py:33
  110.3 27.6 %collective-permute-start.16 = (bf16[1280,512]{1,0:T(8,128)(2,1)}, bf16[1280,512]{1,0:T(8,128)(2,1)S(1)}, u32[]{:S(2)}, u32[]{:S(2)}) collective-permute-start(bf16[1280,512]{1,0:T(8,128)(2,1)} %get-tuple-element.41), channel_id=1, source_target_pairs={{0,32},{8,40},{16,48},{24,56},{32,64},{40,72},{48,80},{56,88},{64,... | collective-permute-start | bytes 3932168 | tf_op jit(solution)/shard_map/ppermute | solution.py:29
  110.3 27.6 %collective-permute-start.17 = (bf16[1280,512]{1,0:T(8,128)(2,1)}, bf16[1280,512]{1,0:T(8,128)(2,1)S(1)}, u32[]{:S(2)}, u32[]{:S(2)}) collective-permute-start(bf16[1280,512]{1,0:T(8,128)(2,1)} %get-tuple-element.42), channel_id=1, source_target_pairs={{0,96},{8,104},{16,112},{24,120},{32,0},{40,8},{48,16},{56,24},{64... | collective-permute-start | bytes 3932168 | tf_op jit(solution)/shard_map/ppermute | solution.py:29
  113.0 27.1 %collective-permute-start.18 = (bf16[1280,512]{1,0:T(8,128)(2,1)}, bf16[1280,512]{1,0:T(8,128)(2,1)}, u32[]{:S(2)}, u32[]{:S(2)}) collective-permute-start(bf16[1280,512]{1,0:T(8,128)(2,1)} %get-tuple-element.43), channel_id=1, source_target_pairs={{0,8},{8,16},{16,24},{24,0},{32,40},{40,48},{48,56},{56,32},{64,72... | collective-permute-start | bytes 3932168 | tf_op jit(solution)/shard_map/ppermute | solution.py:29
  113.0 27.0 %collective-permute-start.19 = (bf16[1280,512]{1,0:T(8,128)(2,1)}, bf16[1280,512]{1,0:T(8,128)(2,1)}, u32[]{:S(2)}, u32[]{:S(2)}) collective-permute-start(bf16[1280,512]{1,0:T(8,128)(2,1)} %get-tuple-element.44), channel_id=1, source_target_pairs={{0,24},{8,0},{16,8},{24,16},{32,56},{40,32},{48,40},{56,48},{64,88... | collective-permute-start | bytes 3932168 | tf_op jit(solution)/shard_map/ppermute | solution.py:29
  151.2 8.6 %collective-permute-start.20 = (bf16[4,10,128,128]{3,2,1,0:T(8,128)(2,1)}, bf16[4,10,128,128]{3,2,1,0:T(8,128)(2,1)S(1)}, u32[]{:S(2)}, u32[]{:S(2)}) collective-permute-start(bf16[4,10,128,128]{3,2,1,0:T(8,128)(2,1)} %get-tuple-element.46), channel_id=1, source_target_pairs={{0,1},{1,0},{2,3},{3,2},{4,5},{5,4},{6,7},{7,6},{8,9},{9,8},{10,11... | collective-permute-start | bytes 3932168 | tf_op jit(solution)/shard_map/ppermute | solution.py:33
  164.9 22.7 %collective-permute-start.21 = (bf16[10,128,128]{2,1,0:T(8,128)(2,1)}, bf16[10,128,128]{2,1,0:T(8,128)(2,1)S(1)}, u32[]{:S(2)}, u32[]{:S(2)}) collective-permute-start(bf16[10,128,128]{2,1,0:T(8,128)(2,1)} %get-tuple-element.47), channel_id=1, source_target_pairs={{0,2},{1,3},{2,4},{3,5},{4,6},{5,7},{6,0},{7,1},{8,10},{9,11},{10,... | collective-permute-start | bytes 983048 | tf_op jit(solution)/shard_map/ppermute | solution.py:33
  165.9 21.7 %collective-permute-start.22 = (bf16[10,128,128]{2,1,0:T(8,128)(2,1)}, bf16[10,128,128]{2,1,0:T(8,128)(2,1)}, u32[]{:S(2)}, u32[]{:S(2)}) collective-permute-start(bf16[10,128,128]{2,1,0:T(8,128)(2,1)} %get-tuple-element.48), channel_id=1, source_target_pairs={{0,6},{1,7},{2,0},{3,1},{4,2},{5,3},{6,4},{7,5},{8,14},{9,15},{10,... | collective-permute-start | bytes 983048 | tf_op jit(solution)/shard_map/ppermute | solution.py:33
  167.7 21.5 %copy-start.5 = (bf16[80,128,128]{2,1,0:T(8,128)(2,1)S(1)}, bf16[80,128,128]{2,1,0:T(8,128)(2,1)}, u32[]{:S(2)}) copy-start(bf16[80,128,128]{2,1,0:T(8,128)(2,1)} %get-tuple-element.45.part_ref) | copy-start | bytes 7864324
  167.7 20.0 %collective-permute-start.23 = (bf16[10,128,128]{2,1,0:T(8,128)(2,1)}, bf16[10,128,128]{2,1,0:T(8,128)(2,1)}, u32[]{:S(2)}, u32[]{:S(2)}) collective-permute-start(bf16[10,128,128]{2,1,0:T(8,128)(2,1)} %get-tuple-element.49), channel_id=1, source_target_pairs={{0,4},{1,5},{2,6},{3,7},{4,0},{5,1},{6,2},{7,3},{8,12},{9,13},{10,... | collective-permute-start | bytes 983048 | tf_op jit(solution)/shard_map/ppermute | solution.py:33
  187.6 8.3 %collective-permute-start.24 = (bf16[4,10,128,384]{3,2,1,0:T(8,128)(2,1)}, bf16[4,10,128,384]{3,2,1,0:T(8,128)(2,1)}, u32[]{:S(2)}, u32[]{:S(2)}) collective-permute-start(bf16[4,10,128,384]{3,2,1,0:T(8,128)(2,1)} %get-tuple-element.54), channel_id=1, source_target_pairs={{0,1},{1,0},{2,3},{3,2},{4,5},{5,4},{6,7},{7,6},{8,9},{9,8},{10,11... | collective-permute-start | bytes 11796488 | tf_op jit(solution)/shard_map/ppermute | solution.py:33
  213.0 2.0 collective-permute-start.28
  215.2 4.4 %collective-permute-start.29 = (bf16[64,512]{1,0:T(8,128)(2,1)S(1)}, bf16[64,512]{1,0:T(8,128)(2,1)S(1)}, u32[]{:S(2)}, u32[]{:S(2)}) collective-permute-start(bf16[64,512]{1,0:T(8,128)(2,1)S(1)} %get-tuple-element.66), channel_id=1, source_target_pairs={{0,2},{1,3},{2,4},{3,5},{4,6},{5,7},{6,0},{7,1},{8,10},{9,11},{10,... | collective-permute-start | bytes 196616 | tf_op jit(solution)/shard_map/ppermute | solution.py:33
  215.7 3.8 %collective-permute-start.30 = (bf16[64,512]{1,0:T(8,128)(2,1)S(1)}, bf16[64,512]{1,0:T(8,128)(2,1)S(1)}, u32[]{:S(2)}, u32[]{:S(2)}) collective-permute-start(bf16[64,512]{1,0:T(8,128)(2,1)S(1)} %get-tuple-element.68), channel_id=1, source_target_pairs={{0,6},{1,7},{2,0},{3,1},{4,2},{5,3},{6,4},{7,5},{8,14},{9,15},{10,... | collective-permute-start | bytes 196616 | tf_op jit(solution)/shard_map/ppermute | solution.py:33
  217.9 4.6 %collective-permute-start.31 = (bf16[64,512]{1,0:T(8,128)(2,1)S(1)}, bf16[64,512]{1,0:T(8,128)(2,1)S(1)}, u32[]{:S(2)}, u32[]{:S(2)}) collective-permute-start(bf16[64,512]{1,0:T(8,128)(2,1)S(1)} %get-tuple-element.67), channel_id=1, source_target_pairs={{0,4},{1,5},{2,6},{3,7},{4,0},{5,1},{6,2},{7,3},{8,12},{9,13},{10,... | collective-permute-start | bytes 196616 | tf_op jit(solution)/shard_map/ppermute | solution.py:33
  222.6 6.5 %collective-permute-start.32 = (bf16[64,512]{1,0:T(8,128)(2,1)S(1)}, bf16[64,512]{1,0:T(8,128)(2,1)S(1)}, u32[]{:S(2)}, u32[]{:S(2)}) collective-permute-start(bf16[64,512]{1,0:T(8,128)(2,1)S(1)} %fusion.13), channel_id=1, source_target_pairs={{0,64},{8,72},{16,80},{24,88},{32,96},{40,104},{48,112},{56,120},{... | collective-permute-start | bytes 196616 | tf_op jit(solution)/shard_map/ppermute | solution.py:29
  223.5 5.5 %collective-permute-start.33 = (bf16[64,512]{1,0:T(8,128)(2,1)S(1)}, bf16[64,512]{1,0:T(8,128)(2,1)S(1)}, u32[]{:S(2)}, u32[]{:S(2)}) collective-permute-start(bf16[64,512]{1,0:T(8,128)(2,1)S(1)} %fusion.13), channel_id=1, source_target_pairs={{0,32},{8,40},{16,48},{24,56},{32,64},{40,72},{48,80},{56,88},{64,... | collective-permute-start | bytes 196616 | tf_op jit(solution)/shard_map/ppermute | solution.py:29
  224.4 4.6 %collective-permute-start.34 = (bf16[64,512]{1,0:T(8,128)(2,1)S(1)}, bf16[64,512]{1,0:T(8,128)(2,1)S(1)}, u32[]{:S(2)}, u32[]{:S(2)}) collective-permute-start(bf16[64,512]{1,0:T(8,128)(2,1)S(1)} %fusion.13), channel_id=1, source_target_pairs={{0,96},{8,104},{16,112},{24,120},{32,0},{40,8},{48,16},{56,24},{64... | collective-permute-start | bytes 196616 | tf_op jit(solution)/shard_map/ppermute | solution.py:29
  226.3 21.8 %collective-permute-start.25 = (bf16[10,128,384]{2,1,0:T(8,128)(2,1)}, bf16[10,128,384]{2,1,0:T(8,128)(2,1)S(1)}, u32[]{:S(2)}, u32[]{:S(2)}) collective-permute-start(bf16[10,128,384]{2,1,0:T(8,128)(2,1)} %get-tuple-element.55), channel_id=1, source_target_pairs={{0,2},{1,3},{2,4},{3,5},{4,6},{5,7},{6,0},{7,1},{8,10},{9,11},{10,... | collective-permute-start | bytes 2949128 | tf_op jit(solution)/shard_map/ppermute | solution.py:33
  226.3 21.7 %collective-permute-start.26 = (bf16[10,128,384]{2,1,0:T(8,128)(2,1)}, bf16[10,128,384]{2,1,0:T(8,128)(2,1)S(1)}, u32[]{:S(2)}, u32[]{:S(2)}) collective-permute-start(bf16[10,128,384]{2,1,0:T(8,128)(2,1)} %get-tuple-element.56), channel_id=1, source_target_pairs={{0,6},{1,7},{2,0},{3,1},{4,2},{5,3},{6,4},{7,5},{8,14},{9,15},{10,... | collective-permute-start | bytes 2949128 | tf_op jit(solution)/shard_map/ppermute | solution.py:33
  229.0 40.2 %collective-permute-start.27 = (bf16[10,128,384]{2,1,0:T(8,128)(2,1)}, bf16[10,128,384]{2,1,0:T(8,128)(2,1)S(1)}, u32[]{:S(2)}, u32[]{:S(2)}) collective-permute-start(bf16[10,128,384]{2,1,0:T(8,128)(2,1)} %get-tuple-element.57), channel_id=1, source_target_pairs={{0,4},{1,5},{2,6},{3,7},{4,0},{5,1},{6,2},{7,3},{8,12},{9,13},{10,... | collective-permute-start | bytes 2949128 | tf_op jit(solution)/shard_map/ppermute | solution.py:33
  229.1 4.9 %collective-permute-start.35 = (bf16[64,512]{1,0:T(8,128)(2,1)S(1)}, bf16[64,512]{1,0:T(8,128)(2,1)S(1)}, u32[]{:S(2)}, u32[]{:S(2)}) collective-permute-start(bf16[64,512]{1,0:T(8,128)(2,1)S(1)} %add_convert_fusion), channel_id=1, source_target_pairs={{0,16},{8,24},{16,0},{24,8},{32,48},{40,56},{48,32},{56,40},{64,80... | collective-permute-start | bytes 196616 | tf_op jit(solution)/shard_map/ppermute | solution.py:29
  231.8 4.9 %collective-permute-start.36 = (bf16[64,512]{1,0:T(8,128)(2,1)S(1)}, bf16[64,512]{1,0:T(8,128)(2,1)S(1)}, u32[]{:S(2)}, u32[]{:S(2)}) collective-permute-start(bf16[64,512]{1,0:T(8,128)(2,1)S(1)} %add_convert_fusion), channel_id=1, source_target_pairs={{0,8},{8,16},{16,24},{24,0},{32,40},{40,48},{48,56},{56,32},{64,72... | collective-permute-start | bytes 196616 | tf_op jit(solution)/shard_map/ppermute | solution.py:29
  233.9 4.0 %collective-permute-start.37 = (bf16[64,512]{1,0:T(8,128)(2,1)S(1)}, bf16[64,512]{1,0:T(8,128)(2,1)S(1)}, u32[]{:S(2)}, u32[]{:S(2)}) collective-permute-start(bf16[64,512]{1,0:T(8,128)(2,1)S(1)} %add_convert_fusion), channel_id=1, source_target_pairs={{0,24},{8,0},{16,8},{24,16},{32,56},{40,32},{48,40},{56,48},{64,88... | collective-permute-start | bytes 196616 | tf_op jit(solution)/shard_map/ppermute | solution.py:29
  269.2 5.0 %collective-permute-start.38 = (f32[64,512]{1,0:T(8,128)S(1)}, f32[64,512]{1,0:T(8,128)S(1)}, u32[]{:S(2)}, u32[]{:S(2)}) collective-permute-start(f32[64,512]{1,0:T(8,128)S(1)} %add_add_fusion), channel_id=1, source_target_pairs={{0,2},{1,3},{2,4},{3,5},{4,6},{5,7},{6,0},{7,1},{8,10},{9,11},{10,... | collective-permute-start | bytes 393224 | tf_op jit(solution)/shard_map/ppermute | solution.py:33
  269.7 5.5 %collective-permute-start.39 = (f32[64,512]{1,0:T(8,128)S(1)}, f32[64,512]{1,0:T(8,128)S(1)}, u32[]{:S(2)}, u32[]{:S(2)}) collective-permute-start(f32[64,512]{1,0:T(8,128)S(1)} %add_add_fusion), channel_id=1, source_target_pairs={{0,6},{1,7},{2,0},{3,1},{4,2},{5,3},{6,4},{7,5},{8,14},{9,15},{10,... | collective-permute-start | bytes 393224 | tf_op jit(solution)/shard_map/ppermute | solution.py:33
  271.9 5.3 %collective-permute-start.40 = (f32[64,512]{1,0:T(8,128)S(1)}, f32[64,512]{1,0:T(8,128)S(1)}, u32[]{:S(2)}, u32[]{:S(2)}) collective-permute-start(f32[64,512]{1,0:T(8,128)S(1)} %add_add_fusion), channel_id=1, source_target_pairs={{0,4},{1,5},{2,6},{3,7},{4,0},{5,1},{6,2},{7,3},{8,12},{9,13},{10,... | collective-permute-start | bytes 393224 | tf_op jit(solution)/shard_map/ppermute | solution.py:33
  277.2 7.8 %collective-permute-start.41 = (f32[256,512]{1,0:T(8,128)S(1)}, f32[256,512]{1,0:T(8,128)S(1)}, u32[]{:S(2)}, u32[]{:S(2)}) collective-permute-start(f32[256,512]{1,0:T(8,128)S(1)} %bitcast.73), channel_id=1, source_target_pairs={{0,1},{1,0},{2,3},{3,2},{4,5},{5,4},{6,7},{7,6},{8,9},{9,8},{10,11... | collective-permute-start | bytes 1572872 | tf_op jit(solution)/shard_map/ppermute | solution.py:33
  (8 other events, 61.8 us)
Sparse Core Ops, SparseCore 0:
  9.7 63.9 all-gather.1
where the time goes:
time: 294 us; the launch traced here: 293 us
  waiting for transfers between devices  101 us (34%)
  starting transfers between devices  68.6 us (23%)
  Pallas kernels  61 us (21%)
  matrix products  18.4 us (6%)
  other arithmetic  17.3 us (6%)
  between operations  14.4 us (5%)
  local copies, waits for them, and re-layouts  12.2 us (4%)
    ppermute x20, waiting for transfers between devices, rep_send(): return lax.ppermute(value, 'rep', perm)  51.4 us
    ppermute x22, waiting for transfers between devices, rows_send(): return lax.ppermute(value, 'rows', perm)  49 us
    ppermute x20, starting transfers between devices, rep_send(): return lax.ppermute(value, 'rep', perm)  35.5 us
    ppermute x22, starting transfers between devices, rows_send(): return lax.ppermute(value, 'rows', perm)  33.1 us
    pallas_call x2, Pallas kernels, product_call(): pl.pallas_call(functools.partial(product_kernel, per_step=per_step, group...  29.6 us
    dot_general x2, matrix products, local(): lax.dot_general(scaled, late.reshape(-1, chunk), (((0,), (0,)), ((), ()))...  16.5 us
    pallas_call x1, Pallas kernels, prep_call(): pl.pallas_call(functools.partial(prep_kernel, per_step=per_step), grid_sp...  13.4 us
    convert_element_type x1, other arithmetic, local(): (block_features.astype(F32) * (scale.reshape(-1, 1) * norm)).astype(BF16)  10.6 us
  transfers between devices with their start and end apart: 43, of which 19 were waited for; matrix products, arithmetic and copies ran while one was open for 12% of the time, Pallas kernels for 14%

commit v1 on v0

--- a/solution.py
+++ b/solution.py
@@ -99,11 +99,11 @@
     def copy_in(part, j, k):
         own, below, above, far_plus, far_minus = pieces[5 * part : 5 * part + 5]
         if j < 3:
-            source, at = (own, below, above)[j], k * half
+            source, at, column = (own, below, above)[j], k * half, begin
         else:
-            source, at = (far_plus, far_minus)[k // 2], k % 2 * half
+            source, at, column = (far_plus, far_minus)[k // 2], k % 2 * half, 0
         z, x = (j, k) if part == 0 else (k, j)
-        source = source.at[pl.ds(at, half), pl.ds(begin, width)]
+        source = source.at[pl.ds(at, half), pl.ds(column, width)]
         return pltpu.make_async_copy(source, held.at[z, x, pl.ds(part * half, half)], sem.at[part, z, x])
 
     @pl.when(step == 0)
@@ -178,26 +178,29 @@
 
 
 def halves_kernel(*refs):
-    for source, target in zip(refs[:4], refs[4:]):
-        target[...] = source[...]
+    sources, targets = refs[:4], refs[4:]
+    for i, target in enumerate(targets):
+        begin, width = CHUNKS[i // 4]
+        target[...] = sources[i % 4][:, begin : begin + width]
 
 
 def halves_call(*four):
     rows, width = four[0].shape
     steps = 4
-    block = (rows // 2 // steps, width)
-    low = pl.BlockSpec(block, lambda g: (g, 0))
-    high = pl.BlockSpec(block, lambda g: (g + steps, 0))
-    return pl.pallas_call(
+    block = rows // 2 // steps
+    low = pl.BlockSpec((block, width), lambda g: (g, 0))
+    high = pl.BlockSpec((block, width), lambda g: (g + steps, 0))
+    made = pl.pallas_call(
         halves_kernel,
         grid=(steps,),
         in_specs=[low, high, low, high],
-        out_specs=[low] * 4,
-        out_shape=[jax.ShapeDtypeStruct((rows // 2, width), BF16)] * 4,
+        out_specs=[pl.BlockSpec((block, chunk), lambda g: (g, 0)) for _, chunk in CHUNKS for _ in range(4)],
+        out_shape=[jax.ShapeDtypeStruct((rows // 2, chunk), BF16) for _, chunk in CHUNKS for _ in range(4)],
         compiler_params=pltpu.CompilerParams(vmem_limit_bytes=VMEM_LIMIT),
         cost_estimate=SMALL,
         name="halves",
     )(*four)
+    return [made[4 * i : 4 * i + 4] for i in range(len(CHUNKS))]
 
 
 def pack_kernel(place_ref, part_ref, got_ref, *out_refs):
@@ -251,13 +254,12 @@
     mine = lax.dynamic_index_in_dim(halves, core, 0, keepdims=False)
     value = mine + rep_send(other, CORE)
     along_y = (YP, YM, Y2)
-    value = value.reshape(4, rows // 8, -1)
+    value = after(value, beside).reshape(4, rows // 8, -1)
     take = lambda i: lax.dynamic_index_in_dim(value, i % 4, 0, keepdims=False)
     parts = [rep_send(take(y + d).astype(BF16), p) for d, p in zip((1, 3, 2), along_y)]
     value = take(y) + parts[0].astype(F32) + parts[1].astype(F32) + parts[2].astype(F32)
     value = exchange_axis(value, rows_send, (ZP, ZM, Z2))
     value = exchange_axis(value, rows_send, (XP, XM, X2))
-    value = after(value, beside)
     value = gather_axis(value, y, rep_send, along_y)
     got = rep_send(value, CORE)
     low = jnp.where(core == 0, value, got)
@@ -302,8 +304,10 @@
 
     first = [jnp.concatenate(spread(upper, XP, XM, values)), jnp.concatenate(spread(lower, ZP, ZM, values))]
     near = [rows_send(v, p) for v, ways in zip(first, ((ZP, ZM), (XP, XM))) for p in ways]
-    far = [rows_send(v, p) for v, p in zip(halves_call(*near), (ZP, ZM, XP, XM))]
-    pieces = [first[0], *near[:2], *far[:2], first[1], *near[2:], *far[2:]]
+    pieces = []
+    for four in halves_call(*near):
+        far = [rows_send(v, p) for v, p in zip(four, (ZP, ZM, XP, XM))]
+        pieces.append([first[0], *near[:2], *far[:2], first[1], *near[2:], *far[2:]])
 
     degree = degree[:, 0]
     degree = degree + rep_send(degree, CORE)
@@ -313,27 +317,36 @@
     norm = 1.0 / jnp.sqrt(jnp.float32(total_verts))
     scaled = (block_features.astype(F32) * (scale.reshape(-1, 1) * norm)).astype(BF16)
 
-    sums, terms = [], []
-    previous = (scaled, own_scale)
-    for i, (begin, chunk) in enumerate(CHUNKS):
-        made = product_call(after(index, previous), groups, values, pieces, row_count, begin, chunk)
-        if i:
-            made = after(made, sums[-1][2:])
-        part, send = made
-        got = rep_send(send, CORE)
+    def multiply(i, *previous):
+        return product_call(
+            after(index, previous), groups, values, pieces[i], row_count, *CHUNKS[i]
+        )
+
+    def term_of(part):
+        return lax.dot_general(
+            scaled,
+            part.reshape(-1, part.shape[-1]),
+            (((0,), (0,)), ((), ())),
+            preferred_element_type=F32,
+        )
+
+    def along_rep(part, got):
         packed = pack_call(groups, part, got)
-        sums.append([part, got] + [rep_send(v, p) for v, p in zip(packed, (YP, YM, Y2))])
-        late = after(part, packed) if i else part
-        terms.append(
-            lax.dot_general(
-                scaled,
-                late.reshape(-1, chunk),
-                (((0,), (0,)), ((), ())),
-                preferred_element_type=F32,
-            )
-        )
-        previous = packed
-    weight_grad = reduce_all(jnp.concatenate(terms, axis=1), core, y, sums[-1][2:])
+        return packed, [rep_send(v, p) for v, p in zip(packed, (YP, YM, Y2))]
+
+    part_a, send_a = after(multiply(0, scaled, own_scale), pieces[1])
+    got_a = rep_send(send_a, CORE)
+    term_a = term_of(part_a)
+    part_b, send_b = multiply(1, term_a, got_a)
+    got_b = rep_send(send_b, CORE)
+    got_a = after(got_a, part_b)
+    packed_a, moved_a = along_rep(part_a, got_a)
+    got_b = after(got_b, packed_a)
+    packed_b, moved_b = along_rep(part_b, got_b)
+    term_b = term_of(after(part_b, packed_b, moved_a))
+    terms = [term_a, term_b]
+    sums = [[part_a, got_a, *moved_a], [part_b, got_b, *moved_b]]
+    weight_grad = reduce_all(jnp.concatenate(terms, axis=1), core, y, moved_b)
 
     aggregated = []
     for part, got, below, above, far in sums:

time: 294 us -> 293 us (level)
  waiting for transfers between devices: 101 us -> 91.7 us
  starting transfers between devices: 68.6 us -> 74.8 us
    ppermute x20, waiting for transfers between devices: 51.4 us -> 44.6 us  [rep_send(): return lax.ppermute(value, 'rep', perm)]
    ppermute x20, starting transfers between devices: 35.5 us -> 41.4 us  [rep_send(): return lax.ppermute(value, 'rep', perm)]
    ppermute x22 -> x26, waiting for transfers between devices: 49 us -> 46.4 us  [rows_send(): return lax.ppermute(value, 'rows', perm)]
    unnamed x33 -> x41, local copies, waits for them, and re-layouts: 7.38 us -> 7.82 us
    ppermute x22 -> x26, starting transfers between devices: 33.1 us -> 33.3 us  [rows_send(): return lax.ppermute(value, 'rows', perm)]
  transfers between devices with their start and end apart: 43 -> 47, of which waited for: 19 -> 16; matrix products, arithmetic and copies ran while one was open for 12% -> 16% of each run, Pallas kernels for 14% -> 15%
where the time goes in v1:
time: 293 us
  waiting for transfers between devices  91.7 us (31%)
  starting transfers between devices  74.8 us (26%)
  Pallas kernels  61 us (21%)
  matrix products  19.9 us (7%)
  other arithmetic  18.2 us (6%)
  between operations  14.5 us (5%)
  local copies, waits for them, and re-layouts  12.6 us (4%)
    ppermute x26, waiting for transfers between devices, rows_send(): return lax.ppermute(value, 'rows', perm)  46.4 us
    ppermute x20, waiting for transfers between devices, rep_send(): return lax.ppermute(value, 'rep', perm)  44.6 us
    ppermute x20, starting transfers between devices, rep_send(): return lax.ppermute(value, 'rep', perm)  41.4 us
    ppermute x26, starting transfers between devices, rows_send(): return lax.ppermute(value, 'rows', perm)  33.3 us
    pallas_call x2, Pallas kernels, product_call(): pl.pallas_call(functools.partial(product_kernel, per_step=per_step, group...  29.6 us
    dot_general x2, matrix products, term_of(): lax.dot_general(scaled, part.reshape(-1, part.shape[-1]), (((0,), (0,)),...  17.9 us
    pallas_call x1, Pallas kernels, prep_call(): pl.pallas_call(functools.partial(prep_kernel, per_step=per_step), grid_sp...  13.3 us
    convert_element_type x1, other arithmetic, local(): (block_features.astype(F32) * (scale.reshape(-1, 1) * norm)).astype(BF16)  10.6 us
  transfers between devices with their start and end apart: 47, of which 16 were waited for; matrix products, arithmetic and copies ran while one was open for 16% of the time, Pallas kernels for 15%

profile of v1, /device:TPU:1, one launch (start us, length us, event | category | flops | bytes accessed | tf_op | source)
XLA Modules:
  0.0 292.8 jit_solution(9272344978012178562)
XLA Ops:
  7.9 3.0 %mask.1 = (bf16[640,512]{1,0:T(8,128)(2,1)}, bf16[640,512]{1,0:T(8,128)(2,1)}) custom-call(bf16[1280,512]{1,0:T(8,128)(2,1)} %grad_ref.1, bf16[1280,512]{1,0:T(8,128)(2,1)} %act_ref.1), custom_call_target="tpu_custom_call" | custom-call | bytes 65536 | tf_op jit(solution)/shard_map/mask/pallas_call | solution.py:45
  10.9 2.5 collective-permute-start.10
  13.4 2.1 collective-permute-start.11
  16.7 1.5 collective-permute-start.5
  18.8 13.3 %prep.1 = (bf16[288,128,128]{2,1,0:T(8,128)(2,1)}, f32[80,8,128]{2,1,0:T(8,128)}) custom-call(s32[288]{0:T(512)} %reshape_squeeze.3.row_ref, s32[288,128,128]{2,1,0:T(8,128)} %bitcast.64), custom_call_target="tpu_custom_call" | custom-call | bytes 65536 | tf_op jit(solution)/shard_map/prep/pallas_call | solution.py:72
  33.5 2.7 collective-permute-start.13
  36.6 2.5 collective-permute-start.7
  44.7 2.2 collective-permute-start.15
  48.4 2.7 collective-permute-start.9
  52.1 3.9 %collective-permute-start = (f32[80,128]{1,0:T(8,128)S(1)}, f32[80,128]{1,0:T(8,128)S(1)}, u32[]{:S(2)}, u32[]{:S(2)}) collective-permute-start(f32[80,128]{1,0:T(8,128)S(1)} %bitcast.72), channel_id=1, source_target_pairs={{0,1},{1,0},{2,3},{3,2},{4,5},{5,4},{6,7},{7,6},{8,9},{9,8},{10,11... | collective-permute-start | bytes 122888 | tf_op jit(solution)/shard_map/ppermute | solution.py:33
  57.8 3.0 %collective-permute-start.1 = (f32[80,128]{1,0:T(8,128)S(1)}, f32[80,128]{1,0:T(8,128)S(1)}, u32[]{:S(2)}, u32[]{:S(2)}) collective-permute-start(f32[80,128]{1,0:T(8,128)S(1)} %add.212), channel_id=1, source_target_pairs={{0,4},{1,5},{2,6},{3,7},{4,0},{5,1},{6,2},{7,3},{8,12},{9,13},{10,... | collective-permute-start | bytes 122888 | tf_op jit(solution)/shard_map/ppermute | solution.py:33
  60.7 40.7 %collective-permute-done.14.refs_2_.refs_6_ = bf16[2560,512]{1,0:T(8,128)(2,1)S(1)} collective-permute-done((bf16[2560,512]{1,0:T(8,128)(2,1)}, bf16[2560,512]{1,0:T(8,128)(2,1)S(1)}, u32[]{:S(2)}, u32[]{:S(2)}) %collective-permute-start.14) | collective-permute-done | bytes 2621472 | tf_op jit(solution)/shard_map/ppermute | solution.py:29
  102.5 1.8 collective-permute-start.3
  105.1 5.3 %halves.1 = (bf16[1280,128]{1,0:T(8,128)(2,1)}, bf16[1280,128]{1,0:T(8,128)(2,1)}, bf16[1280,128]{1,0:T(8,128)(2,1)}, bf16[1280,128]{1,0:T(8,128)(2,1)}, bf16[12...) custom-call(bf16[2560,512]{1,0:T(8,128)(2,1)} %collective-permute-done.8., ...), custom_call_target="tpu_custom_call" | custom-call | bytes 65536 | tf_op jit(solution)/shard_map/halves/pallas_call | solution.py:193
  110.5 2.7 collective-permute-start.17
  113.2 2.7 collective-permute-start.19
  116.0 1.9 collective-permute-done.16.refs_3_
  120.8 1.6 collective-permute-start.23
  122.5 10.6 %multiply_convert_fusion = bf16[10240,512]{1,0:T(8,128)(2,1)} fusion(bf16[10240,512]{1,0:T(8,128)(2,1)} %all-gather.2.cloned.1.call-done, f32[10240]{0:T(1024)S(1)} %get-tuple-element.74), kind=kLoop, calls=%fused_computation.1 | loop fusion | flops 15728640 | bytes 21012480 | tf_op jit(solution)/shard_map/convert_element_type | solution.py:318
  133.1 11.1 %product.2 = (bf16[80,128,128]{2,1,0:T(8,128)(2,1)}, bf16[4,10,128,128]{3,2,1,0:T(8,128)(2,1)}) custom-call(s32[3,288]{1,0:T(4,128)} %pad_add_fusion.index_ref, s32[12]{0:T(128)} %pad_add_fusion.1.place_ref, bf16[288,128,128]{2,1,0:T(8,128)(2,1)} %get-tuple-element.42.values_ref, bf16[2560,512]{1,0:T(8,128)(2,1)} %constant_dynamic-update-slice_fusion.refs_0_, ...), custom_call_target="tpu_custom_call" | custom-call | bytes 65536 | tf_op jit(solution)/shard_map/product/pallas_call | solution.py:152
  144.3 10.0 %collective-permute-start.24 = (bf16[4,10,128,128]{3,2,1,0:T(8,128)(2,1)}, bf16[4,10,128,128]{3,2,1,0:T(8,128)(2,1)S(1)}, u32[]{:S(2)}, u32[]{:S(2)}) collective-permute-start(bf16[4,10,128,128]{3,2,1,0:T(8,128)(2,1)} %get-tuple-element.58), channel_id=1, source_target_pairs={{0,1},{1,0},{2,3},{3,2},{4,5},{5,4},{6,7},{7,6},{8,9},{9,8},{10,11... | collective-permute-start | bytes 3932168 | tf_op jit(solution)/shard_map/ppermute | solution.py:33
  154.2 7.1 %fusion.25 = f32[512,128]{0,1:T(8,128)} fusion(bf16[10240,512]{1,0:T(8,128)(2,1)} %multiply_convert_fusion, bf16[10240,128]{1,0:T(8,128)(2,1)} %bitcast.68), kind=kOutput, calls=%fused_computation.76 | convolution fusion | flops 1342177280 | bytes 13369344 | tf_op jit(solution)/shard_map/dot_general | solution.py:326
  161.4 18.5 %product.3 = (bf16[80,128,384]{2,1,0:T(8,128)(2,1)}, bf16[4,10,128,384]{3,2,1,0:T(8,128)(2,1)}) custom-call(s32[3,288]{1,0:T(4,128)} %pad_add_fusion.index_ref, s32[12]{0:T(128)} %pad_add_fusion.1.place_ref, bf16[288,128,128]{2,1,0:T(8,128)(2,1)} %get-tuple-element.42.values_ref, bf16[2560,512]{1,0:T(8,128)(2,1)} %constant_dynamic-update-slice_fusion.refs_0_, ...), custom_call_target="tpu_custom_call" | custom-call | bytes 65536 | tf_op jit(solution)/shard_map/product/pallas_call | solution.py:152
  180.9 4.0 %pack.2 = (bf16[10,128,128]{2,1,0:T(8,128)(2,1)}, bf16[10,128,128]{2,1,0:T(8,128)(2,1)}, bf16[10,128,128]{2,1,0:T(8,128)(2,1)}) custom-call(s32[12]{0:T(128)} %pad_add_fusion.1.place_ref, bf16[80,128,128]{2,1,0:T(8,128)(2,1)} %get-tuple-element.57.part_ref, bf16[4,10,128,128]{3,2,1,0:T(8,128)(2,1)} %copy-done.3), custom_call_target="tpu_custom_call" | custom-call | bytes 65536 | tf_op jit(solution)/shard_map/pack/pallas_call | solution.py:218
  186.1 1.5 collective-permute-start.26
  187.6 1.6 collective-permute-start.27
  189.2 5.8 %pack.3 = (bf16[10,128,384]{2,1,0:T(8,128)(2,1)}, bf16[10,128,384]{2,1,0:T(8,128)(2,1)}, bf16[10,128,384]{2,1,0:T(8,128)(2,1)}) custom-call(s32[12]{0:T(128)} %pad_add_fusion.1.place_ref, bf16[80,128,384]{2,1,0:T(8,128)(2,1)} %get-tuple-element.70.part_ref, bf16[4,10,128,384]{3,2,1,0:T(8,128)(2,1)} %collective-permute-done.28.got_ref), custom_call_target="tpu_custom_call" | custom-call | bytes 65536 | tf_op jit(solution)/shard_map/pack/pallas_call | solution.py:218
  195.5 2.3 collective-permute-start.30
  197.9 6.0 %collective-permute-done.27 = bf16[10,128,128]{2,1,0:T(8,128)(2,1)S(1)} collective-permute-done((bf16[10,128,128]{2,1,0:T(8,128)(2,1)}, bf16[10,128,128]{2,1,0:T(8,128)(2,1)S(1)}, u32[]{:S(2)}, u32[]{:S(2)}) %collective-permute-start.27) | collective-permute-done | bytes 327712 | tf_op jit(solution)/shard_map/ppermute | solution.py:33
  204.6 10.8 %fusion.26 = f32[512,384]{0,1:T(8,128)S(1)} fusion(bf16[10240,512]{1,0:T(8,128)(2,1)} %multiply_convert_fusion, bf16[10240,384]{1,0:T(8,128)(2,1)} %bitcast.65), kind=kOutput, calls=%fused_computation.77 | convolution fusion | flops 4026531840 | bytes 19136512 | tf_op jit(solution)/shard_map/dot_general | solution.py:326
  215.9 1.3 collective-permute-start.32
  217.2 1.5 collective-permute-done.32
  218.9 6.7 %collective-permute-done.29 = bf16[10,128,384]{2,1,0:T(8,128)(2,1)} collective-permute-done((bf16[10,128,384]{2,1,0:T(8,128)(2,1)}, bf16[10,128,384]{2,1,0:T(8,128)(2,1)}, u32[]{:S(2)}, u32[]{:S(2)}) %collective-permute-start.29) | collective-permute-done | bytes 983072 | tf_op jit(solution)/shard_map/ppermute | solution.py:33
  225.6 20.5 %collective-permute-done.31 = bf16[10,128,384]{2,1,0:T(8,128)(2,1)} collective-permute-done((bf16[10,128,384]{2,1,0:T(8,128)(2,1)}, bf16[10,128,384]{2,1,0:T(8,128)(2,1)}, u32[]{:S(2)}, u32[]{:S(2)}) %collective-permute-start.31) | collective-permute-done | bytes 983072 | tf_op jit(solution)/shard_map/ppermute | solution.py:33
  246.8 2.1 collective-permute-start.34
  249.1 1.4 collective-permute-done.33
  250.6 3.0 %collective-permute-done.35 = bf16[64,512]{1,0:T(8,128)(2,1)S(1)} collective-permute-done((bf16[64,512]{1,0:T(8,128)(2,1)S(1)}, bf16[64,512]{1,0:T(8,128)(2,1)S(1)}, u32[]{:S(2)}, u32[]{:S(2)}) %collective-permute-start.35) | collective-permute-done | bytes 65568 | tf_op jit(solution)/shard_map/ppermute | solution.py:33
  253.6 1.3 collective-permute-start.36
  254.8 2.7 collective-permute-start.38
  257.5 1.4 fusion.9
  259.6 2.6 collective-permute-start.41
  262.4 1.7 collective-permute-done.39
  264.7 3.0 %fusion.2 = f32[10,128,384]{2,1,0:T(8,128)S(1)} fusion(bf16[10,128,384]{2,1,0:T(8,128)(2,1)} %collective-permute-done.31, bf16[10,128,384]{2,1,0:T(8,128)(2,1)} %collective-permute-done.30, bf16[10,128,384]{2,1,0:T(8,128)(2,1)} %collective-permute-done.29, bf16[4,10,128,384]{3,2,1,0:T(8,128)(2,1)} %collective-permute-done.28.got_ref, ...), kind=kLoop, calls=%fused_computation.6 | loop fusion | flops 4423680 | bytes 6881284 | tf_op jit(solution)/shard_map/add | solution.py:354
  267.7 2.7 collective-permute-start.43
  270.5 3.3 %collective-permute-done.43 = f32[64,512]{1,0:T(8,128)S(1)} collective-permute-done((f32[64,512]{1,0:T(8,128)S(1)}, f32[64,512]{1,0:T(8,128)S(1)}, u32[]{:S(2)}, u32[]{:S(2)}) %collective-permute-start.43) | collective-permute-done | bytes 131104 | tf_op jit(solution)/shard_map/ppermute | solution.py:33
  273.8 2.1 collective-permute-done.44
  275.9 6.7 %collective-permute-start.45 = (f32[256,512]{1,0:T(8,128)S(1)}, f32[256,512]{1,0:T(8,128)S(1)}, u32[]{:S(2)}, u32[]{:S(2)}) collective-permute-start(f32[256,512]{1,0:T(8,128)S(1)} %bitcast.69), channel_id=1, source_target_pairs={{0,1},{1,0},{2,3},{3,2},{4,5},{5,4},{6,7},{7,6},{8,9},{9,8},{10,11... | collective-permute-start | bytes 1572872 | tf_op jit(solution)/shard_map/ppermute | solution.py:33
  282.8 2.0 convolution_convert_fusion
  (140 shorter events, 26.8 us)
Async XLA Ops:
  7.2 275.6 %copy-start = (bf16[512,512]{1,0:T(8,128)(2,1)S(1)}, bf16[512,512]{1,0:T(8,128)(2,1)}, u32[]{:S(2)}) copy-start(bf16[512,512]{1,0:T(8,128)(2,1)} %param.13) | copy-start | bytes 1572868
  7.2 115.3 %all-gather.2.cloned.1.call-start = ((), (), s32[]{:S(2)}) async-start(), calls=%async_computation | async-start | bytes 11796480 | tf_op jit(solution)/shard_map/all_gather | solution.py:284
  10.9 22.5 %collective-permute-start.10 = (bf16[640,512]{1,0:T(8,128)(2,1)}, bf16[640,512]{1,0:T(8,128)(2,1)S(1)}, u32[]{:S(2)}, u32[]{:S(2)}) collective-permute-start(bf16[640,512]{1,0:T(8,128)(2,1)} %get-tuple-element.38), channel_id=1, source_target_pairs={{0,32},{8,40},{16,48},{24,56},{32,64},{40,72},{48,80},{56,88},{64,... | collective-permute-start | bytes 1966088 | tf_op jit(solution)/shard_map/ppermute | solution.py:29
  13.4 20.0 %collective-permute-start.11 = (bf16[640,512]{1,0:T(8,128)(2,1)}, bf16[640,512]{1,0:T(8,128)(2,1)S(1)}, u32[]{:S(2)}, u32[]{:S(2)}) collective-permute-start(bf16[640,512]{1,0:T(8,128)(2,1)} %get-tuple-element.38), channel_id=1, source_target_pairs={{0,96},{8,104},{16,112},{24,120},{32,0},{40,8},{48,16},{56,24},{64... | collective-permute-start | bytes 1966088 | tf_op jit(solution)/shard_map/ppermute | solution.py:29
  15.5 20.7 %collective-permute-start.4 = (bf16[640,512]{1,0:T(8,128)(2,1)}, bf16[640,512]{1,0:T(8,128)(2,1)S(1)}, u32[]{:S(2)}, u32[]{:S(2)}) collective-permute-start(bf16[640,512]{1,0:T(8,128)(2,1)} %get-tuple-element.37), channel_id=1, source_target_pairs={{0,8},{8,16},{16,24},{24,0},{32,40},{40,48},{48,56},{56,32},{64,72... | collective-permute-start | bytes 1966088 | tf_op jit(solution)/shard_map/ppermute | solution.py:29
  16.7 19.5 %collective-permute-start.5 = (bf16[640,512]{1,0:T(8,128)(2,1)}, bf16[640,512]{1,0:T(8,128)(2,1)S(1)}, u32[]{:S(2)}, u32[]{:S(2)}) collective-permute-start(bf16[640,512]{1,0:T(8,128)(2,1)} %get-tuple-element.37), channel_id=1, source_target_pairs={{0,24},{8,0},{16,8},{24,16},{32,56},{40,32},{48,40},{56,48},{64,88... | collective-permute-start | bytes 1966088 | tf_op jit(solution)/shard_map/ppermute | solution.py:29
  33.4 9.3 %collective-permute-start.12 = (bf16[320,512]{1,0:T(8,128)(2,1)S(1)}, bf16[320,512]{1,0:T(8,128)(2,1)S(1)}, u32[]{:S(2)}, u32[]{:S(2)}) collective-permute-start(bf16[320,512]{1,0:T(8,128)(2,1)S(1)} %slice.24), channel_id=1, source_target_pairs={{0,32},{8,40},{16,48},{24,56},{32,64},{40,72},{48,80},{56,88},{64,... | collective-permute-start | bytes 983048 | tf_op jit(solution)/shard_map/ppermute | solution.py:29
  33.5 10.0 %collective-permute-start.13 = (bf16[320,512]{1,0:T(8,128)(2,1)S(1)}, bf16[320,512]{1,0:T(8,128)(2,1)S(1)}, u32[]{:S(2)}, u32[]{:S(2)}) collective-permute-start(bf16[320,512]{1,0:T(8,128)(2,1)S(1)} %slice.25), channel_id=1, source_target_pairs={{0,96},{8,104},{16,112},{24,120},{32,0},{40,8},{48,16},{56,24},{64... | collective-permute-start | bytes 983048 | tf_op jit(solution)/shard_map/ppermute | solution.py:29
  36.3 10.7 %collective-permute-start.6 = (bf16[320,512]{1,0:T(8,128)(2,1)S(1)}, bf16[320,512]{1,0:T(8,128)(2,1)S(1)}, u32[]{:S(2)}, u32[]{:S(2)}) collective-permute-start(bf16[320,512]{1,0:T(8,128)(2,1)S(1)} %slice.22), channel_id=1, source_target_pairs={{0,8},{8,16},{16,24},{24,0},{32,40},{40,48},{48,56},{56,32},{64,72... | collective-permute-start | bytes 983048 | tf_op jit(solution)/shard_map/ppermute | solution.py:29
  36.6 11.0 %collective-permute-start.7 = (bf16[320,512]{1,0:T(8,128)(2,1)S(1)}, bf16[320,512]{1,0:T(8,128)(2,1)S(1)}, u32[]{:S(2)}, u32[]{:S(2)}) collective-permute-start(bf16[320,512]{1,0:T(8,128)(2,1)S(1)} %slice.23), channel_id=1, source_target_pairs={{0,24},{8,0},{16,8},{24,16},{32,56},{40,32},{48,40},{56,48},{64,88... | collective-permute-start | bytes 983048 | tf_op jit(solution)/shard_map/ppermute | solution.py:29
  44.2 57.2 %collective-permute-start.14 = (bf16[2560,512]{1,0:T(8,128)(2,1)}, bf16[2560,512]{1,0:T(8,128)(2,1)S(1)}, u32[]{:S(2)}, u32[]{:S(2)}) collective-permute-start(bf16[2560,512]{1,0:T(8,128)(2,1)} %constant_dynamic-update-slice_fusion.5.refs_5_), channel_id=1, source_target_pairs={{0,8},{8,16},{16,24},{24,0},{32,40},{40,48},{48,56},{56,32},{64,72... | collective-permute-start | bytes 7864328 | tf_op jit(solution)/shard_map/ppermute | solution.py:29
  44.7 57.8 %collective-permute-start.15 = (bf16[2560,512]{1,0:T(8,128)(2,1)}, bf16[2560,512]{1,0:T(8,128)(2,1)}, u32[]{:S(2)}, u32[]{:S(2)}) collective-permute-start(bf16[2560,512]{1,0:T(8,128)(2,1)} %constant_dynamic-update-slice_fusion.5.refs_5_), channel_id=1, source_target_pairs={{0,24},{8,0},{16,8},{24,16},{32,56},{40,32},{48,40},{56,48},{64,88... | collective-permute-start | bytes 7864328 | tf_op jit(solution)/shard_map/ppermute | solution.py:29
  48.4 56.7 %collective-permute-start.8 = (bf16[2560,512]{1,0:T(8,128)(2,1)}, bf16[2560,512]{1,0:T(8,128)(2,1)}, u32[]{:S(2)}, u32[]{:S(2)}) collective-permute-start(bf16[2560,512]{1,0:T(8,128)(2,1)} %constant_dynamic-update-slice_fusion.refs_0_), channel_id=1, source_target_pairs={{0,32},{8,40},{16,48},{24,56},{32,64},{40,72},{48,80},{56,88},{64,... | collective-permute-start | bytes 7864328 | tf_op jit(solution)/shard_map/ppermute | solution.py:29
  48.4 56.7 %collective-permute-start.9 = (bf16[2560,512]{1,0:T(8,128)(2,1)}, bf16[2560,512]{1,0:T(8,128)(2,1)}, u32[]{:S(2)}, u32[]{:S(2)}) collective-permute-start(bf16[2560,512]{1,0:T(8,128)(2,1)} %constant_dynamic-update-slice_fusion.refs_0_), channel_id=1, source_target_pairs={{0,96},{8,104},{16,112},{24,120},{32,0},{40,8},{48,16},{56,24},{64... | collective-permute-start | bytes 7864328 | tf_op jit(solution)/shard_map/ppermute | solution.py:29
  52.1 5.7 %collective-permute-start = (f32[80,128]{1,0:T(8,128)S(1)}, f32[80,128]{1,0:T(8,128)S(1)}, u32[]{:S(2)}, u32[]{:S(2)}) collective-permute-start(f32[80,128]{1,0:T(8,128)S(1)} %bitcast.72), channel_id=1, source_target_pairs={{0,1},{1,0},{2,3},{3,2},{4,5},{5,4},{6,7},{7,6},{8,9},{9,8},{10,11... | collective-permute-start | bytes 122888 | tf_op jit(solution)/shard_map/ppermute | solution.py:33
  57.8 55.4 %collective-permute-start.1 = (f32[80,128]{1,0:T(8,128)S(1)}, f32[80,128]{1,0:T(8,128)S(1)}, u32[]{:S(2)}, u32[]{:S(2)}) collective-permute-start(f32[80,128]{1,0:T(8,128)S(1)} %add.212), channel_id=1, source_target_pairs={{0,4},{1,5},{2,6},{3,7},{4,0},{5,1},{6,2},{7,3},{8,12},{9,13},{10,... | collective-permute-start | bytes 122888 | tf_op jit(solution)/shard_map/ppermute | solution.py:33
  101.5 11.7 %collective-permute-start.2 = (f32[80,128]{1,0:T(8,128)S(1)}, f32[80,128]{1,0:T(8,128)S(1)}, u32[]{:S(2)}, u32[]{:S(2)}) collective-permute-start(f32[80,128]{1,0:T(8,128)S(1)} %add.212), channel_id=1, source_target_pairs={{0,2},{1,3},{2,4},{3,5},{4,6},{5,7},{6,0},{7,1},{8,10},{9,11},{10,... | collective-permute-start | bytes 122888 | tf_op jit(solution)/shard_map/ppermute | solution.py:33
  102.5 10.7 %collective-permute-start.3 = (f32[80,128]{1,0:T(8,128)S(1)}, f32[80,128]{1,0:T(8,128)S(1)}, u32[]{:S(2)}, u32[]{:S(2)}) collective-permute-start(f32[80,128]{1,0:T(8,128)S(1)} %add.212), channel_id=1, source_target_pairs={{0,6},{1,7},{2,0},{3,1},{4,2},{5,3},{6,4},{7,5},{8,14},{9,15},{10,... | collective-permute-start | bytes 122888 | tf_op jit(solution)/shard_map/ppermute | solution.py:33
  110.4 7.4 %collective-permute-start.16 = (bf16[1280,128]{1,0:T(8,128)(2,1)}, bf16[1280,128]{1,0:T(8,128)(2,1)S(1)}, u32[]{:S(2)}, u32[]{:S(2)}) collective-permute-start(bf16[1280,128]{1,0:T(8,128)(2,1)} %get-tuple-element.47), channel_id=1, source_target_pairs={{0,32},{8,40},{16,48},{24,56},{32,64},{40,72},{48,80},{56,88},{64,... | collective-permute-start | bytes 983048 | tf_op jit(solution)/shard_map/ppermute | solution.py:29
  110.5 8.5 %collective-permute-start.17 = (bf16[1280,128]{1,0:T(8,128)(2,1)}, bf16[1280,128]{1,0:T(8,128)(2,1)S(1)}, u32[]{:S(2)}, u32[]{:S(2)}) collective-permute-start(bf16[1280,128]{1,0:T(8,128)(2,1)} %get-tuple-element.48), channel_id=1, source_target_pairs={{0,96},{8,104},{16,112},{24,120},{32,0},{40,8},{48,16},{56,24},{64... | collective-permute-start | bytes 983048 | tf_op jit(solution)/shard_map/ppermute | solution.py:29
  113.2 7.6 %collective-permute-start.18 = (bf16[1280,128]{1,0:T(8,128)(2,1)}, bf16[1280,128]{1,0:T(8,128)(2,1)}, u32[]{:S(2)}, u32[]{:S(2)}) collective-permute-start(bf16[1280,128]{1,0:T(8,128)(2,1)} %get-tuple-element.49), channel_id=1, source_target_pairs={{0,8},{8,16},{16,24},{24,0},{32,40},{40,48},{48,56},{56,32},{64,72... | collective-permute-start | bytes 983048 | tf_op jit(solution)/shard_map/ppermute | solution.py:29
  113.2 19.9 %collective-permute-start.19 = (bf16[1280,128]{1,0:T(8,128)(2,1)}, bf16[1280,128]{1,0:T(8,128)(2,1)}, u32[]{:S(2)}, u32[]{:S(2)}) collective-permute-start(bf16[1280,128]{1,0:T(8,128)(2,1)} %get-tuple-element.50), channel_id=1, source_target_pairs={{0,24},{8,0},{16,8},{24,16},{32,56},{40,32},{48,40},{56,48},{64,88... | collective-permute-start | bytes 983048 | tf_op jit(solution)/shard_map/ppermute | solution.py:29
  116.0 28.2 %collective-permute-start.20 = (bf16[1280,384]{1,0:T(8,128)(2,1)}, bf16[1280,384]{1,0:T(8,128)(2,1)S(1)}, u32[]{:S(2)}, u32[]{:S(2)}) collective-permute-start(bf16[1280,384]{1,0:T(8,128)(2,1)} %get-tuple-element.53), channel_id=1, source_target_pairs={{0,32},{8,40},{16,48},{24,56},{32,64},{40,72},{48,80},{56,88},{64,... | collective-permute-start | bytes 2949128 | tf_op jit(solution)/shard_map/ppermute | solution.py:29
  117.8 26.4 %collective-permute-start.21 = (bf16[1280,384]{1,0:T(8,128)(2,1)}, bf16[1280,384]{1,0:T(8,128)(2,1)S(1)}, u32[]{:S(2)}, u32[]{:S(2)}) collective-permute-start(bf16[1280,384]{1,0:T(8,128)(2,1)} %get-tuple-element.54), channel_id=1, source_target_pairs={{0,96},{8,104},{16,112},{24,120},{32,0},{40,8},{48,16},{56,24},{64... | collective-permute-start | bytes 2949128 | tf_op jit(solution)/shard_map/ppermute | solution.py:29
  119.8 24.4 %collective-permute-start.22 = (bf16[1280,384]{1,0:T(8,128)(2,1)}, bf16[1280,384]{1,0:T(8,128)(2,1)S(1)}, u32[]{:S(2)}, u32[]{:S(2)}) collective-permute-start(bf16[1280,384]{1,0:T(8,128)(2,1)} %get-tuple-element.55), channel_id=1, source_target_pairs={{0,8},{8,16},{16,24},{24,0},{32,40},{40,48},{48,56},{56,32},{64,72... | collective-permute-start | bytes 2949128 | tf_op jit(solution)/shard_map/ppermute | solution.py:29
  120.8 23.4 %collective-permute-start.23 = (bf16[1280,384]{1,0:T(8,128)(2,1)}, bf16[1280,384]{1,0:T(8,128)(2,1)}, u32[]{:S(2)}, u32[]{:S(2)}) collective-permute-start(bf16[1280,384]{1,0:T(8,128)(2,1)} %get-tuple-element.56), channel_id=1, source_target_pairs={{0,24},{8,0},{16,8},{24,16},{32,56},{40,32},{48,40},{56,48},{64,88... | collective-permute-start | bytes 2949128 | tf_op jit(solution)/shard_map/ppermute | solution.py:29
  144.3 17.1 %collective-permute-start.24 = (bf16[4,10,128,128]{3,2,1,0:T(8,128)(2,1)}, bf16[4,10,128,128]{3,2,1,0:T(8,128)(2,1)S(1)}, u32[]{:S(2)}, u32[]{:S(2)}) collective-permute-start(bf16[4,10,128,128]{3,2,1,0:T(8,128)(2,1)} %get-tuple-element.58), channel_id=1, source_target_pairs={{0,1},{1,0},{2,3},{3,2},{4,5},{5,4},{6,7},{7,6},{8,9},{9,8},{10,11... | collective-permute-start | bytes 3932168 | tf_op jit(solution)/shard_map/ppermute | solution.py:33
  179.9 9.3 %collective-permute-start.28 = (bf16[4,10,128,384]{3,2,1,0:T(8,128)(2,1)}, bf16[4,10,128,384]{3,2,1,0:T(8,128)(2,1)}, u32[]{:S(2)}, u32[]{:S(2)}) collective-permute-start(bf16[4,10,128,384]{3,2,1,0:T(8,128)(2,1)} %get-tuple-element.65), channel_id=1, source_target_pairs={{0,1},{1,0},{2,3},{3,2},{4,5},{5,4},{6,7},{7,6},{8,9},{9,8},{10,11... | collective-permute-start | bytes 11796488 | tf_op jit(solution)/shard_map/ppermute | solution.py:33
  184.9 12.8 %collective-permute-start.25 = (bf16[10,128,128]{2,1,0:T(8,128)(2,1)}, bf16[10,128,128]{2,1,0:T(8,128)(2,1)S(1)}, u32[]{:S(2)}, u32[]{:S(2)}) collective-permute-start(bf16[10,128,128]{2,1,0:T(8,128)(2,1)} %get-tuple-element.62), channel_id=1, source_target_pairs={{0,2},{1,3},{2,4},{3,5},{4,6},{5,7},{6,0},{7,1},{8,10},{9,11},{10,... | collective-permute-start | bytes 983048 | tf_op jit(solution)/shard_map/ppermute | solution.py:33
  186.1 11.8 %collective-permute-start.26 = (bf16[10,128,128]{2,1,0:T(8,128)(2,1)}, bf16[10,128,128]{2,1,0:T(8,128)(2,1)S(1)}, u32[]{:S(2)}, u32[]{:S(2)}) collective-permute-start(bf16[10,128,128]{2,1,0:T(8,128)(2,1)} %get-tuple-element.63), channel_id=1, source_target_pairs={{0,6},{1,7},{2,0},{3,1},{4,2},{5,3},{6,4},{7,5},{8,14},{9,15},{10,... | collective-permute-start | bytes 983048 | tf_op jit(solution)/shard_map/ppermute | solution.py:33
  187.6 16.3 %collective-permute-start.27 = (bf16[10,128,128]{2,1,0:T(8,128)(2,1)}, bf16[10,128,128]{2,1,0:T(8,128)(2,1)S(1)}, u32[]{:S(2)}, u32[]{:S(2)}) collective-permute-start(bf16[10,128,128]{2,1,0:T(8,128)(2,1)} %get-tuple-element.64), channel_id=1, source_target_pairs={{0,4},{1,5},{2,6},{3,7},{4,0},{5,1},{6,2},{7,3},{8,12},{9,13},{10,... | collective-permute-start | bytes 983048 | tf_op jit(solution)/shard_map/ppermute | solution.py:33
  195.1 30.5 %collective-permute-start.29 = (bf16[10,128,384]{2,1,0:T(8,128)(2,1)}, bf16[10,128,384]{2,1,0:T(8,128)(2,1)}, u32[]{:S(2)}, u32[]{:S(2)}) collective-permute-start(bf16[10,128,384]{2,1,0:T(8,128)(2,1)} %get-tuple-element.67), channel_id=1, source_target_pairs={{0,2},{1,3},{2,4},{3,5},{4,6},{5,7},{6,0},{7,1},{8,10},{9,11},{10,... | collective-permute-start | bytes 2949128 | tf_op jit(solution)/shard_map/ppermute | solution.py:33
  195.5 30.1 %collective-permute-start.30 = (bf16[10,128,384]{2,1,0:T(8,128)(2,1)}, bf16[10,128,384]{2,1,0:T(8,128)(2,1)}, u32[]{:S(2)}, u32[]{:S(2)}) collective-permute-start(bf16[10,128,384]{2,1,0:T(8,128)(2,1)} %get-tuple-element.68), channel_id=1, source_target_pairs={{0,6},{1,7},{2,0},{3,1},{4,2},{5,3},{6,4},{7,5},{8,14},{9,15},{10,... | collective-permute-start | bytes 2949128 | tf_op jit(solution)/shard_map/ppermute | solution.py:33
  197.7 48.4 %collective-permute-start.31 = (bf16[10,128,384]{2,1,0:T(8,128)(2,1)}, bf16[10,128,384]{2,1,0:T(8,128)(2,1)}, u32[]{:S(2)}, u32[]{:S(2)}) collective-permute-start(bf16[10,128,384]{2,1,0:T(8,128)(2,1)} %get-tuple-element.69), channel_id=1, source_target_pairs={{0,4},{1,5},{2,6},{3,7},{4,0},{5,1},{6,2},{7,3},{8,12},{9,13},{10,... | collective-permute-start | bytes 2949128 | tf_op jit(solution)/shard_map/ppermute | solution.py:33
  215.9 2.8 collective-permute-start.32
  246.2 4.4 %collective-permute-start.33 = (bf16[64,512]{1,0:T(8,128)(2,1)S(1)}, bf16[64,512]{1,0:T(8,128)(2,1)S(1)}, u32[]{:S(2)}, u32[]{:S(2)}) collective-permute-start(bf16[64,512]{1,0:T(8,128)(2,1)S(1)} %get-tuple-element.80), channel_id=1, source_target_pairs={{0,2},{1,3},{2,4},{3,5},{4,6},{5,7},{6,0},{7,1},{8,10},{9,11},{10,... | collective-permute-start | bytes 196616 | tf_op jit(solution)/shard_map/ppermute | solution.py:33
  246.8 3.8 %collective-permute-start.34 = (bf16[64,512]{1,0:T(8,128)(2,1)S(1)}, bf16[64,512]{1,0:T(8,128)(2,1)S(1)}, u32[]{:S(2)}, u32[]{:S(2)}) collective-permute-start(bf16[64,512]{1,0:T(8,128)(2,1)S(1)} %get-tuple-element.82), channel_id=1, source_target_pairs={{0,6},{1,7},{2,0},{3,1},{4,2},{5,3},{6,4},{7,5},{8,14},{9,15},{10,... | collective-permute-start | bytes 196616 | tf_op jit(solution)/shard_map/ppermute | solution.py:33
  248.9 4.6 %collective-permute-start.35 = (bf16[64,512]{1,0:T(8,128)(2,1)S(1)}, bf16[64,512]{1,0:T(8,128)(2,1)S(1)}, u32[]{:S(2)}, u32[]{:S(2)}) collective-permute-start(bf16[64,512]{1,0:T(8,128)(2,1)S(1)} %get-tuple-element.81), channel_id=1, source_target_pairs={{0,4},{1,5},{2,6},{3,7},{4,0},{5,1},{6,2},{7,3},{8,12},{9,13},{10,... | collective-permute-start | bytes 196616 | tf_op jit(solution)/shard_map/ppermute | solution.py:33
  253.6 5.3 %collective-permute-start.36 = (bf16[64,512]{1,0:T(8,128)(2,1)S(1)}, bf16[64,512]{1,0:T(8,128)(2,1)S(1)}, u32[]{:S(2)}, u32[]{:S(2)}) collective-permute-start(bf16[64,512]{1,0:T(8,128)(2,1)S(1)} %fusion.13), channel_id=1, source_target_pairs={{0,64},{8,72},{16,80},{24,88},{32,96},{40,104},{48,112},{56,120},{... | collective-permute-start | bytes 196616 | tf_op jit(solution)/shard_map/ppermute | solution.py:29
  254.8 4.3 %collective-permute-start.37 = (bf16[64,512]{1,0:T(8,128)(2,1)S(1)}, bf16[64,512]{1,0:T(8,128)(2,1)S(1)}, u32[]{:S(2)}, u32[]{:S(2)}) collective-permute-start(bf16[64,512]{1,0:T(8,128)(2,1)S(1)} %fusion.13), channel_id=1, source_target_pairs={{0,32},{8,40},{16,48},{24,56},{32,64},{40,72},{48,80},{56,88},{64,... | collective-permute-start | bytes 196616 | tf_op jit(solution)/shard_map/ppermute | solution.py:29
  254.8 4.4 %collective-permute-start.38 = (bf16[64,512]{1,0:T(8,128)(2,1)S(1)}, bf16[64,512]{1,0:T(8,128)(2,1)S(1)}, u32[]{:S(2)}, u32[]{:S(2)}) collective-permute-start(bf16[64,512]{1,0:T(8,128)(2,1)S(1)} %fusion.13), channel_id=1, source_target_pairs={{0,96},{8,104},{16,112},{24,120},{32,0},{40,8},{48,16},{56,24},{64... | collective-permute-start | bytes 196616 | tf_op jit(solution)/shard_map/ppermute | solution.py:29
  259.3 4.8 %collective-permute-start.39 = (bf16[64,512]{1,0:T(8,128)(2,1)S(1)}, bf16[64,512]{1,0:T(8,128)(2,1)S(1)}, u32[]{:S(2)}, u32[]{:S(2)}) collective-permute-start(bf16[64,512]{1,0:T(8,128)(2,1)S(1)} %add_convert_fusion), channel_id=1, source_target_pairs={{0,16},{8,24},{16,0},{24,8},{32,48},{40,56},{48,32},{56,40},{64,80... | collective-permute-start | bytes 196616 | tf_op jit(solution)/shard_map/ppermute | solution.py:29
  259.4 5.1 %collective-permute-start.40 = (bf16[64,512]{1,0:T(8,128)(2,1)S(1)}, bf16[64,512]{1,0:T(8,128)(2,1)S(1)}, u32[]{:S(2)}, u32[]{:S(2)}) collective-permute-start(bf16[64,512]{1,0:T(8,128)(2,1)S(1)} %add_convert_fusion), channel_id=1, source_target_pairs={{0,8},{8,16},{16,24},{24,0},{32,40},{40,48},{48,56},{56,32},{64,72... | collective-permute-start | bytes 196616 | tf_op jit(solution)/shard_map/ppermute | solution.py:29
  259.6 4.9 %collective-permute-start.41 = (bf16[64,512]{1,0:T(8,128)(2,1)S(1)}, bf16[64,512]{1,0:T(8,128)(2,1)S(1)}, u32[]{:S(2)}, u32[]{:S(2)}) collective-permute-start(bf16[64,512]{1,0:T(8,128)(2,1)S(1)} %add_convert_fusion), channel_id=1, source_target_pairs={{0,24},{8,0},{16,8},{24,16},{32,56},{40,32},{48,40},{56,48},{64,88... | collective-permute-start | bytes 196616 | tf_op jit(solution)/shard_map/ppermute | solution.py:29
  264.6 5.9 %collective-permute-start.42 = (f32[64,512]{1,0:T(8,128)S(1)}, f32[64,512]{1,0:T(8,128)S(1)}, u32[]{:S(2)}, u32[]{:S(2)}) collective-permute-start(f32[64,512]{1,0:T(8,128)S(1)} %get-tuple-element.73), channel_id=1, source_target_pairs={{0,2},{1,3},{2,4},{3,5},{4,6},{5,7},{6,0},{7,1},{8,10},{9,11},{10,... | collective-permute-start | bytes 393224 | tf_op jit(solution)/shard_map/ppermute | solution.py:33
  267.7 6.0 %collective-permute-start.43 = (f32[64,512]{1,0:T(8,128)S(1)}, f32[64,512]{1,0:T(8,128)S(1)}, u32[]{:S(2)}, u32[]{:S(2)}) collective-permute-start(f32[64,512]{1,0:T(8,128)S(1)} %get-tuple-element.73), channel_id=1, source_target_pairs={{0,6},{1,7},{2,0},{3,1},{4,2},{5,3},{6,4},{7,5},{8,14},{9,15},{10,... | collective-permute-start | bytes 393224 | tf_op jit(solution)/shard_map/ppermute | solution.py:33
  270.5 5.4 %collective-permute-start.44 = (f32[64,512]{1,0:T(8,128)S(1)}, f32[64,512]{1,0:T(8,128)S(1)}, u32[]{:S(2)}, u32[]{:S(2)}) collective-permute-start(f32[64,512]{1,0:T(8,128)S(1)} %get-tuple-element.73), channel_id=1, source_target_pairs={{0,4},{1,5},{2,6},{3,7},{4,0},{5,1},{6,2},{7,3},{8,12},{9,13},{10,... | collective-permute-start | bytes 393224 | tf_op jit(solution)/shard_map/ppermute | solution.py:33
  275.9 8.9 %collective-permute-start.45 = (f32[256,512]{1,0:T(8,128)S(1)}, f32[256,512]{1,0:T(8,128)S(1)}, u32[]{:S(2)}, u32[]{:S(2)}) collective-permute-start(f32[256,512]{1,0:T(8,128)S(1)} %bitcast.69), channel_id=1, source_target_pairs={{0,1},{1,0},{2,3},{3,2},{4,5},{5,4},{6,7},{7,6},{8,9},{9,8},{10,11... | collective-permute-start | bytes 1572872 | tf_op jit(solution)/shard_map/ppermute | solution.py:33
  (16 other events, 185.8 us)
Sparse Core Ops, SparseCore 0:
  9.7 63.0 all-gather.1
